TPU v7x, 32 devices: a whole 2x2x4 slice. The times are simulated.
32 devices in a mesh: row: 4 (over y, x), col: 8 (over z, core).
Axes of the slice: x: 2, y: 2, z: 4, core: 2. Of those that a mesh axis runs over, the one named last changes fastest.
Arguments:
- hidden: bfloat16 [5120, 5120], P('col'), may hold values from -26 to 26
- lengths: int32 [4], replicated, may hold values from 512 to 2048, as said below
- owner: int32 [4], replicated, may hold values from 0 to 7, as said below
- page_table: int32 [4, 16], replicated, may hold values from 0 to 15, as said below
- qkv_train: float32 [3, 5120, 3072], P(None, 'row', 'col'), may hold values from -1 to 1
- qk_gain: float32 [2, 3072], P(None, 'row'), may hold values from 0.1 to 1.9
- o_weight: bfloat16 [3072, 5120], P('row'), may hold values from -1.5 to 1.5
- post_gain: float32 [5120], P('row'), may hold values from 0.1 to 1.9
- gate_up_train: float32 [2, 5120, 13824], P(None, 'row', 'col'), may hold values from -0.078125 to 0.078125
Outputs:
- layer_out: bfloat16 [5120, 5120], P('col', 'row')
- kv_cache: bfloat16 [8, 16, 2, 128, 3072], P('col', None, None, None, 'row')
- qkv_server: bfloat16 [3, 4, 1280, 3072], P(None, None, 'col', 'row')
- gate_up_server: bfloat16 [2, 4, 1280, 13824], P(None, None, 'col', 'row')
Inputs may be any that keep to these rules, and one draw needn't show every extreme that they name: The lengths add up to 5120; one prompt has 2048 tokens and one 512. `owner`: the owners are distinct. `page_table`: each row is a permutation of the 16 slots.
All inputs are finite; a program needn't handle non-finite values.
Results may differ from a plain program's by a relative error of at most 0.025.
Values may be sent and summed in bfloat16 or wider, within the bound.
No kernel may reach another device: no remote copies, remote signals or barrier semaphores. Data moves between devices by JAX's collectives and lax.ppermute only.
A program may use at most 256 MiB of HBM per device.

v0:
```python
import functools
import math

import jax
import jax.numpy as jnp
from jax import lax
from jax.experimental import pallas as pl
from jax.experimental.pallas import tpu as pltpu
from jax.sharding import PartitionSpec as P

HD = 128
PAGE = 128
PAGES = 16
BOTH = ("row", "col")

norm_epsilon = 1e-06
rope_theta = 500000.0
big_negative = -1e30


def inverse_rms(squares, features):
    return lax.rsqrt(squares / features + norm_epsilon)


def permute(x, n_row, n_col, target):
    pairs = []
    for r in range(n_row):
        for c in range(n_col):
            r2, c2 = target(r, c)
            pairs.append((r * n_col + c, r2 * n_col + c2))
    return lax.ppermute(x, BOTH, pairs)


def after(x, *others):
    return lax.optimization_barrier((x,) + others)[0]


def pick(x, index, axis=0):
    return lax.dynamic_index_in_dim(x, index, axis, keepdims=False)


class Grid:
    def __init__(self):
        self.n_row = lax.axis_size("row")
        self.n_col = lax.axis_size("col")
        self.planes = self.n_col // 2
        self.row = lax.axis_index("row")
        self.col = lax.axis_index("col")
        self.plane = self.col // 2
        self.core = self.col % 2

    def move(self, x, target):
        return permute(x, self.n_row, self.n_col, target)

    def other_core(self, x):
        return self.move(x, lambda r, c: (r, c ^ 1))

    def row_xor(self, x, i):
        return self.move(x, lambda r, c: (r ^ i, c))

    def gather_row(self, x):
        if self.n_row != 4:
            return [x] + [self.row_xor(x, i) for i in range(1, self.n_row)]
        half = x.shape[0] // 2
        first = self.row_xor(x, 1)
        second = self.row_xor(x, 2)
        third = jnp.concatenate(
            [self.row_xor(first[:half], 2), self.row_xor(second[half:], 1)], axis=0
        )
        return [x, first, second, third]

    def across(self, block, i):
        return self.move(block, lambda r, c: (r, (((c // 2) ^ i ^ r) * 2) + c % 2))

    def down(self, block, i):
        return self.move(block, lambda r, c: ((c // 2) ^ i ^ r, c))

    def join_cores(self, mine, other, axis):
        return jnp.where(
            self.core == 0,
            jnp.concatenate([mine, other], axis=axis),
            jnp.concatenate([other, mine], axis=axis),
        )


def attend_kernel(pieces, tokens, piece_tokens, heads, prompts, info, q_ref, *refs):
    kv_refs, out_ref = refs[:pieces], refs[pieces]
    block = pl.program_id(0)
    rows = q_ref.shape[1]
    width = heads * HD
    scale = math.log2(math.e) / math.sqrt(HD)
    first = block * tokens + info[prompts]
    first_start = jnp.int32(0)
    row_id = first + lax.broadcasted_iota(jnp.int32, (rows, 1), 0)
    row_start = jnp.zeros((rows, 1), jnp.int32)
    for p in range(prompts):
        end = info[p]
        first_start = jnp.where(end <= first, jnp.maximum(first_start, end), first_start)
        row_start = jnp.where(end <= row_id, jnp.maximum(row_start, end), row_start)
    lowest = first_start // tokens
    lane = lax.broadcasted_iota(jnp.int32, (1, tokens), 1)
    place = lane + info[prompts + 1]
    for i in range(1, pieces):
        place = jnp.where(
            lane >= i * piece_tokens, lane + (info[prompts + 1 + i] - i * piece_tokens), place
        )
    for head in range(heads):
        at = head * HD
        query = q_ref[0, :, at : at + HD]

        def step(chunk, state):
            top, total, acc = state
            keys = jnp.concatenate([ref[chunk, :, at : at + HD] for ref in kv_refs], axis=0)
            values = jnp.concatenate(
                [ref[chunk, :, width + at : width + at + HD] for ref in kv_refs], axis=0
            )
            scores = lax.dot_general(
                query, keys, (((1,), (1,)), ((), ())), preferred_element_type=jnp.float32
            )
            key_id = chunk * tokens + place
            allowed = (key_id <= row_id) & (key_id >= row_start)
            scores = jnp.where(allowed, scores, big_negative)
            new_top = jnp.maximum(top, jnp.max(scores, axis=1, keepdims=True))
            shrink = jnp.exp2((top - new_top) * scale)
            weights = jnp.exp2((scores - new_top) * scale)
            total = total * shrink + jnp.sum(weights, axis=1, keepdims=True)
            acc = acc * shrink + jnp.dot(
                weights.astype(jnp.bfloat16), values, preferred_element_type=jnp.float32
            )
            return new_top, total, acc

        state = (
            jnp.full((rows, 1), big_negative, jnp.float32),
            jnp.zeros((rows, 1), jnp.float32),
            jnp.zeros((rows, HD), jnp.float32),
        )
        top, total, acc = lax.fori_loop(lowest, block + 1, step, state)
        out_ref[0, :, at : at + HD] = (acc / total).astype(out_ref.dtype)


def attend(query, kv_pieces, info, tokens, prompts):
    blocks, rows, width = query.shape
    pieces = len(kv_pieces)
    piece_tokens = kv_pieces[0].shape[1]
    kernel = functools.partial(
        attend_kernel, pieces, tokens, piece_tokens, width // HD, prompts
    )
    return pl.pallas_call(
        kernel,
        grid_spec=pltpu.PrefetchScalarGridSpec(
            num_scalar_prefetch=1,
            grid=(blocks,),
            in_specs=[pl.BlockSpec((1, rows, width), lambda b, info: (b, 0, 0))]
            + [pl.BlockSpec(x.shape, lambda b, info: (0, 0, 0)) for x in kv_pieces],
            out_specs=pl.BlockSpec((1, rows, width), lambda b, info: (b, 0, 0)),
        ),
        out_shape=jax.ShapeDtypeStruct(query.shape, jnp.bfloat16),
        compiler_params=pltpu.CompilerParams(vmem_limit_bytes=48 * 1024 * 1024),
        cost_estimate=pl.CostEstimate(
            flops=4 * blocks * rows * width * tokens * 3,
            bytes_accessed=4 * blocks * rows * width + 2 * sum(x.size for x in kv_pieces),
            transcendentals=blocks * rows * (width // HD) * tokens * 3,
        ),
        name="attend",
    )(info, query, *kv_pieces)


def page_kernel(info, pages_ref, out_ref):
    page = info[pl.program_id(0)]
    row = page * PAGE + lax.broadcasted_iota(jnp.int32, (1, PAGE, 1), 1)
    inside = row < info[PAGES]
    out_ref[0] = jnp.where(inside, pages_ref[0].astype(jnp.float32), 0.0).astype(out_ref.dtype)


def place_pages(pages, info):
    shape = pages.shape
    spec = (1,) + shape[1:]
    return pl.pallas_call(
        page_kernel,
        grid_spec=pltpu.PrefetchScalarGridSpec(
            num_scalar_prefetch=1,
            grid=(PAGES,),
            in_specs=[pl.BlockSpec(spec, lambda s, info: (info[s], 0, 0, 0))],
            out_specs=pl.BlockSpec(spec, lambda s, info: (s, 0, 0, 0)),
        ),
        out_shape=jax.ShapeDtypeStruct(shape, pages.dtype),
        cost_estimate=pl.CostEstimate(
            flops=pages.size, bytes_accessed=4 * pages.size, transcendentals=0
        ),
        name="place_pages",
    )(info, pages)


def local(
    hidden, lengths, owner, page_table, qkv_train, qk_gain, o_weight, post_gain, gate_up_train
):
    grid = Grid()
    n_row, n_col, planes = grid.n_row, grid.n_col, grid.planes
    row, col, plane, core = grid.row, grid.col, grid.plane, grid.core
    bf16 = jnp.bfloat16
    prompts = lengths.shape[0]
    tokens, width = hidden.shape
    part = tokens // n_row
    row_width = width // n_row
    col_block = row_width // n_col
    units = qkv_train.shape[2]
    heads_width = units * n_col
    ff_units = gate_up_train.shape[2]

    prompt_ends = jnp.cumsum(lengths)
    prompt_starts = prompt_ends - lengths

    quarter = lax.dynamic_slice_in_dim(hidden, row * part, part, 0).reshape(part, n_row, row_width)
    quarter = jnp.concatenate([pick(quarter, row ^ i, 1) for i in range(n_row)], axis=1)
    gathered = lax.all_gather(quarter, "col", axis=0, tiled=True)
    weights = qkv_train.astype(bf16).transpose(1, 0, 2).reshape(row_width, 3 * units)
    weight_pieces = grid.gather_row(weights)
    gain = pick(lax.all_gather(qk_gain, "row", axis=0), plane)
    whole_heads = units % HD == 0
    held = units if whole_heads else 2 * units
    if whole_heads:
        gain = lax.dynamic_slice_in_dim(gain, core * units, units, 1)

    projected = 0.0
    for i in range(n_row):
        projected = projected + jnp.dot(
            gathered[:, i * row_width : (i + 1) * row_width],
            weight_pieces[i],
            preferred_element_type=jnp.float32,
        )
    rows_here = n_col * part
    projected = projected.reshape(rows_here, 3, units)
    squares = jnp.sum(projected[:, :2] * projected[:, :2], axis=2)
    squares = jnp.sum(lax.all_gather(squares.T, "col", axis=0), axis=0)
    inverse = inverse_rms(squares, heads_width)
    if not whole_heads:
        projected = grid.join_cores(projected, grid.other_core(projected), 2)

    token = (
        jnp.arange(n_col, dtype=jnp.int32)[:, None] * tokens
        + row * part
        + jnp.arange(part, dtype=jnp.int32)[None, :]
    ).reshape(rows_here)
    start = jnp.max(jnp.where(token[:, None] >= prompt_ends[None, :], prompt_ends[None, :], 0), axis=1)
    position = token - start
    half = HD // 2
    frequency = rope_theta ** (-2.0 * jnp.arange(half, dtype=jnp.float32) / HD)
    angles = position.astype(jnp.float32)[:, None] * frequency[None, :]
    cosine = jnp.cos(angles)
    sine = jnp.sin(angles)
    cosine = jnp.concatenate([cosine, cosine], axis=1)[:, None, :]
    sine = jnp.concatenate([-sine, sine], axis=1)[:, None, :]

    def rotate(x):
        x = x.reshape(rows_here, held // HD, HD)
        swapped = jnp.concatenate([x[..., half:], x[..., :half]], axis=-1)
        return (x * cosine + swapped * sine).reshape(rows_here, held).astype(bf16)

    query = rotate(projected[:, 0] * inverse[0][:, None] * gain[0])
    key = rotate(projected[:, 1] * inverse[1][:, None] * gain[1])
    value = projected[:, 2].astype(bf16)
    kv = jnp.concatenate([key, value], axis=1)

    kv_pieces = [x.reshape(n_col, part, 2 * held) for x in grid.gather_row(kv)]
    offsets = jnp.stack([(row ^ i) * part for i in range(n_row)])
    if part % 16:
        stacked = jnp.stack(kv_pieces)
        natural = jnp.stack([pick(stacked, row ^ r) for r in range(n_row)], axis=1)
        kv_pieces = [natural.reshape(n_col, tokens, 2 * held)]
        offsets = jnp.zeros((1,), jnp.int32)
    info = jnp.concatenate([prompt_ends, (row * part)[None], offsets]).astype(jnp.int32)
    attention = attend(query.reshape(n_col, part, held), kv_pieces, info, tokens, prompts)

    attention = attention.reshape(planes, 2, part, held)
    mine = pick(attention, core, 1)
    if whole_heads:
        attention = grid.join_cores(mine, grid.other_core(pick(attention, 1 - core, 1)), 2)
    else:
        attention = mine
    arrived = jnp.stack(
        [
            grid.down(grid.across(pick(attention, plane ^ i ^ row), i), i)
            for i in range(n_row)
        ]
    )
    attention_rows = jnp.concatenate(
        [pick(arrived, r ^ row ^ plane) for r in range(n_row)], axis=0
    )
    partial_out = jnp.dot(attention_rows, o_weight, preferred_element_type=jnp.float32).astype(bf16)
    partial_out = partial_out.reshape(tokens, n_row, row_width)
    summed = pick(partial_out, row, 1).astype(jnp.float32)
    for i in range(1, n_row):
        summed = summed + grid.row_xor(pick(partial_out, row ^ i, 1), i).astype(jnp.float32)
    out_squares = lax.psum(jnp.sum(summed * summed, axis=1), "row")
    normalized = summed * inverse_rms(out_squares, width)[:, None] * post_gain
    residual = lax.dynamic_slice_in_dim(hidden, row * row_width, row_width, 1).astype(jnp.float32)
    layer_out = (residual + normalized).astype(bf16)

    if not whole_heads:
        kv = jnp.concatenate(
            [lax.dynamic_slice_in_dim(x, core * units, units, 1) for x in (key, value)], axis=1
        )
    same_core = [list(range(k, n_col, 2)) for k in range(2)]
    kv_planes = lax.all_gather(kv, "col", axis=0, axis_index_groups=same_core)
    cache_pieces = [pick(kv_planes, row)] + [
        grid.row_xor(pick(kv_planes, row ^ i), i) for i in range(1, n_row)
    ]
    stacked = jnp.stack(cache_pieces).reshape(n_row, n_col, part, 2 * units)
    natural = jnp.stack([pick(stacked, row ^ r) for r in range(n_row)], axis=1)
    natural = natural.reshape(n_col * tokens, 2 * units)
    most = PAGES * PAGE
    natural = jnp.concatenate([natural, jnp.zeros((most, 2 * units), bf16)], axis=0)

    def start_of(owner_col):
        return jnp.sum(jnp.where(owner == owner_col, prompt_starts, 0))

    window_other = grid.other_core(
        lax.dynamic_slice_in_dim(natural, start_of(col ^ 1), most, 0)
    )
    window = lax.dynamic_slice_in_dim(natural, start_of(col), most, 0)
    pages = grid.join_cores(
        window.reshape(PAGES, PAGE, 2, units), window_other.reshape(PAGES, PAGE, 2, units), 3
    ).transpose(0, 2, 1, 3)
    mine = owner == col
    my_length = jnp.sum(jnp.where(mine, lengths, 0))
    my_table = jnp.sum(jnp.where(mine[:, None], page_table, 0), axis=0)
    page_index = jnp.arange(PAGES, dtype=jnp.int32)
    page_of_slot = jnp.sum(
        jnp.where(my_table[None, :] == page_index[:, None], page_index[None, :], 0), axis=1
    )
    page_of_slot = jnp.where(jnp.any(mine), page_of_slot, 0)
    cache = place_pages(pages, jnp.concatenate([page_of_slot, my_length[None]]).astype(jnp.int32))

    def swap_cores(blocks):
        other = grid.other_core(pick(blocks, 1 - core, 1))
        return pick(blocks, core, 1), other

    qkv_mine, qkv_other = swap_cores(weights.reshape(planes, 2, col_block, 3, units))
    qkv_blocks = grid.join_cores(qkv_mine, qkv_other, 3).reshape(planes, col_block, 6 * units)
    ff = gate_up_train.astype(bf16).reshape(2, planes, 2, col_block, ff_units)
    ff_blocks = [grid.join_cores(*swap_cores(ff[j]), 2) for j in range(2)]

    split = 2 if (col_block // 2) % 16 == 0 else 1
    step_rows = col_block // split
    chunks = [(b, s * step_rows) for b in ff_blocks for s in range(split)]
    chunks.append((qkv_blocks, None))
    results = []
    gate = gathered
    for blocks, at in chunks:
        sent = []
        for i in range(n_row):
            block = pick(blocks, plane ^ i ^ row)
            if at is not None:
                block = block[at : at + step_rows]
            sent.append(grid.across(after(block, gate), i))
        gate = sent[0][:8, :128]
        results.append(
            jnp.stack([grid.down(x, i) for i, x in enumerate(sent)])
        )

    def in_order(rounds):
        return jnp.stack([pick(rounds, r ^ row ^ plane) for r in range(n_row)])

    qkv_server = in_order(results[-1]).reshape(n_row, col_block, 3, 2 * units).transpose(2, 0, 1, 3)
    ff_server = [
        jnp.concatenate([in_order(x) for x in results[j * split : (j + 1) * split]], axis=1)
        for j in range(2)
    ]
    return (layer_out, cache[None], qkv_server, jnp.stack(ff_server))


def solution(mesh):
    in_specs = (
        P("col", None),
        P(),
        P(),
        P(),
        P(None, "row", "col"),
        P(None, "row"),
        P("row", None),
        P("row"),
        P(None, "row", "col"),
    )
    out_specs = (
        P("col", "row"),
        P("col", None, None, None, "row"),
        P(None, None, "col", "row"),
        P(None, None, "col", "row"),
    )
    return jax.shard_map(local, mesh=mesh, in_specs=in_specs, out_specs=out_specs, check_vma=False)
```

profile of v0, /device:TPU:16, one launch (start us, length us, event | category | flops | bytes accessed | tf_op | source)
XLA Modules:
  0.0 1024.9 jit_solution(10997872949412044315)
XLA Ops:
  31.7 15.3 %copy.160 = bf16[2,1280,1728]{2,1,0:T(8,128)(2,1)} copy(f32[2,1280,1728]{1,2,0:T(8,128)} %param.17) | data formatting | bytes 26542080 | tf_op args[8]
  59.5 32.3 %all-gather.4 = f32[4,2,768]{2,1,0:T(2,128)S(1)} all-gather(f32[1,2,768]{2,1,0:T(2,128)S(1)} %bitcast.246), channel_id=3, replica_groups=mesh['row'=4,'col'=8] {'row'}, dimensions={0}, use_global_device_ids=true | all-gather | bytes 30720 | tf_op jit(solution)/shard_map/all_gather | solution.py:218
  98.9 36.7 %all-gather.8.cloned.1.call-done = bf16[1280,5120]{1,0:T(8,128)(2,1)} async-done(((bf16[160,5120]{1,0:T(8,128)(2,1)}), bf16[1280,5120]{1,0:T(8,128)(2,1)}) %all-gather.8.cloned.1.call-update) | async-done | bytes 13107216 | tf_op jit(solution)/shard_map/all_gather | solution.py:215
  142.6 8.6 convolution_add_fusion.1
  151.3 8.6 fusion.3
  171.5 13.9 %all-gather.3 = f32[8,2,1280]{2,1,0:T(2,128)S(1)} all-gather(f32[1,2,1280]{2,1,0:T(2,128)S(1)} %bitcast.243), channel_id=2, replica_groups=mesh['row'=4,'col'=8] {'col'}, dimensions={0}, use_global_device_ids=true | all-gather | bytes 92160 | tf_op jit(solution)/shard_map/all_gather | solution.py:234
  244.6 47.9 %collective-permute-done.44 = bf16[80,3456]{1,0:T(8,128)(2,1)} collective-permute-done((bf16[80,3456]{1,0:T(8,128)(2,1)S(1)}, bf16[80,3456]{1,0:T(8,128)(2,1)}, u32[]{:S(2)}, u32[]{:S(2)}) %collective-permute-start.44) | collective-permute-done | bytes 552992 | tf_op jit(solution)/shard_map/ppermute | solution.py:31
  294.4 63.5 %collective-permute-done.42 = bf16[80,3456]{1,0:T(8,128)(2,1)S(1)} collective-permute-done((bf16[80,3456]{1,0:T(8,128)(2,1)S(1)}, bf16[80,3456]{1,0:T(8,128)(2,1)S(1)}, u32[]{:S(2)}, u32[]{:S(2)}) %collective-permute-start.42) | collective-permute-done | bytes 552992 | tf_op jit(solution)/shard_map/ppermute | solution.py:31
  396.1 25.0 %collective-permute-done.49 = bf16[80,3456]{1,0:T(8,128)(2,1)} collective-permute-done((bf16[80,3456]{1,0:T(8,128)(2,1)}, bf16[80,3456]{1,0:T(8,128)(2,1)}, u32[]{:S(2)}, u32[]{:S(2)}) %collective-permute-start.49) | collective-permute-done | bytes 552992 | tf_op jit(solution)/shard_map/ppermute | solution.py:31
  461.1 47.9 %collective-permute-start.58 = (bf16[80,3456]{1,0:T(8,128)(2,1)S(1)}, bf16[80,3456]{1,0:T(8,128)(2,1)}, u32[]{:S(2)}, u32[]{:S(2)}) collective-permute-start(bf16[80,3456]{1,0:T(8,128)(2,1)S(1)} %copy-done.20), channel_id=1, source_target_pairs={{0,6},{1,7},{2,4},{3,5},{4,2},{5,3},{6,0},{7,1},{8,12},{9,13},{10,... | collective-permute-start | bytes 1658888 | tf_op jit(solution)/shard_map/ppermute | solution.py:31
  515.0 30.9 %collective-permute-done.58 = bf16[80,3456]{1,0:T(8,128)(2,1)} collective-permute-done((bf16[80,3456]{1,0:T(8,128)(2,1)S(1)}, bf16[80,3456]{1,0:T(8,128)(2,1)}, u32[]{:S(2)}, u32[]{:S(2)}) %collective-permute-start.58) | collective-permute-done | bytes 552992 | tf_op jit(solution)/shard_map/ppermute | solution.py:31
  601.8 26.7 %collective-permute-done.65 = bf16[80,3456]{1,0:T(8,128)(2,1)} collective-permute-done((bf16[80,3456]{1,0:T(8,128)(2,1)}, bf16[80,3456]{1,0:T(8,128)(2,1)}, u32[]{:S(2)}, u32[]{:S(2)}) %collective-permute-start.65) | collective-permute-done | bytes 552992 | tf_op jit(solution)/shard_map/ppermute | solution.py:31
  631.3 20.7 %collective-permute-done.63 = bf16[80,3456]{1,0:T(8,128)(2,1)} collective-permute-done((bf16[80,3456]{1,0:T(8,128)(2,1)}, bf16[80,3456]{1,0:T(8,128)(2,1)}, u32[]{:S(2)}, u32[]{:S(2)}) %collective-permute-start.63) | collective-permute-done | bytes 552992 | tf_op jit(solution)/shard_map/ppermute | solution.py:31
  674.0 32.5 %attend.1 = bf16[8,160,384]{2,1,0:T(8,128)(2,1)S(1)} custom-call(s32[9]{0:T(128)S(1)} %concatenate.76.info, bf16[8,160,384]{2,1,0:T(8,128)(2,1)S(1)} %get-tuple-element.138.q_ref, bf16[8,160,768]{2,1,0:T(8,128)(2,1)S(1)} %pad_maximum_fusion.9.refs_0_, bf16[8,160,768]{2,1,0:T(8,128)(2,1)S(1)} %bitcast.206, bf16[8,160,768]{2,1,0:T(8,128)(2,1)} %bitcast.230, ...), custom_call_target="tpu_custom_call" | custom-call | flops 3774873600 | bytes 9830400 | tf_op jit(solution)/shard_map/attend/pallas_call | solution.py:148
  720.7 9.6 collective-permute-done.15
  750.1 10.6 %copy.168 = bf16[5120,768]{1,0:T(8,128)(2,1)} copy(bf16[5120,768]{0,1:T(8,128)(2,1)} %all-gather.10.cloned.1.call-done) | data formatting | bytes 15728640 | tf_op jit(solution)/shard_map/all_gather | solution.py:304
  772.2 11.4 %convolution_convert_fusion = bf16[640,5120]{1,0:T(8,128)(2,1)} fusion(bf16[768,5120]{1,0:T(8,128)(2,1)} %param.15, bf16[160,768]{1,0:T(8,128)(2,1)S(1)} %get-tuple-element.148, bf16[160,768]{1,0:T(8,128)(2,1)S(1)} %get-tuple-element.149, bf16[160,768]{1,0:T(8,128)(2,1)S(1)} %get-tuple-element.150, bf16[160,768]{1,0:T(8,128)(2,1)S(1)} %get-tuple-element.147), kind=kOutput, calls=%fused_computation.6 | convolution fusion | flops 5040373760 | bytes 15400960 | tf_op jit(solution)/shard_map/dot_general | solution.py:289
  783.5 12.5 %reshape.238 = bf16[640,4,1280]{2,1,0:T(4,128)(2,1)} reshape(bf16[640,5120]{1,0:T(8,128)(2,1)} %convolution_convert_fusion) | data formatting | bytes 13107200 | tf_op jit(solution)/shard_map/reshape | solution.py:290
  808.2 19.9 %constant_dynamic-slice_fusion.27 = (bf16[640,1,1280]{2,1,0:T(2,128)(2,1)S(1)}, bf16[640,1,1280]{2,1,0:T(2,128)(2,1)S(1)}, bf16[640,1,1280]{2,1,0:T(2,128)(2,1)S(1)}, bf16[640,1,1280]{2,1,0:T(2,128)(2,1)S(1)}) fusion(bf16[640,4,1280]{2,1,0:T(4,128)(2,1)} %reshape.238, s32[]{:T(128)S(6)} %select_n.217, s32[]{:T(128)S(6)} %select_n.219, s32[]{:T(128)S(6)} %select_n.218, ...), kind=kLoop, calls=%fused_computation.148 | loop fusion | bytes 13107216 | tf_op jit(solution)/shard_map/jit(dynamic_index_in_dim)/dynamic_slice | solution.py:39
  835.9 32.3 %collective-permute-start.34 = (bf16[160,2304]{1,0:T(8,128)(2,1)S(1)}, bf16[160,2304]{1,0:T(8,128)(2,1)}, u32[]{:S(2)}, u32[]{:S(2)}) collective-permute-start(bf16[160,2304]{1,0:T(8,128)(2,1)S(1)} %collective-permute-done.33), channel_id=1, source_target_pairs={{0,8},{1,9},{2,2},{3,3},{4,28},{5,29},{6,22},{7,23},{8,0},{9,1},{1... | collective-permute-start | bytes 2211848 | tf_op jit(solution)/shard_map/ppermute | solution.py:31
  896.2 42.0 %collective-permute-done.32 = bf16[160,2304]{1,0:T(8,128)(2,1)} collective-permute-done((bf16[160,2304]{1,0:T(8,128)(2,1)}, bf16[160,2304]{1,0:T(8,128)(2,1)}, u32[]{:S(2)}, u32[]{:S(2)}) %collective-permute-start.32) | collective-permute-done | bytes 737312 | tf_op jit(solution)/shard_map/ppermute | solution.py:31
  953.8 19.0 %collective-permute-done.18 = bf16[640,1280]{1,0:T(8,128)(2,1)} collective-permute-done((bf16[640,1280]{1,0:T(8,128)(2,1)}, bf16[640,1280]{1,0:T(8,128)(2,1)}, u32[]{:S(2)}, u32[]{:S(2)}) %collective-permute-start.18) | collective-permute-done | bytes 1638432 | tf_op jit(solution)/shard_map/ppermute | solution.py:31
  976.2 8.5 psum.7
  1009.5 8.3 place_pages.1
  (315 shorter events, 420.6 us)
Async XLA Ops:
  7.2 128.4 %all-gather.8.cloned.1.call-start = ((), (), s32[]{:S(2)}) async-start(), calls=%async_computation | async-start | bytes 14745600 | tf_op jit(solution)/shard_map/all_gather | solution.py:215
  15.1 735.0 %all-gather.10.cloned.1.call-start = ((), (), s32[]{:S(2)}) async-start(), calls=%async_computation.1 | async-start | bytes 9830400 | tf_op jit(solution)/shard_map/all_gather | solution.py:304
  21.4 71.2 %collective-permute-start.1 = (bf16[1280,1152]{0,1:T(8,128)(2,1)}, bf16[1280,1152]{0,1:T(8,128)(2,1)}, u32[]{:S(2)}, u32[]{:S(2)}) collective-permute-start(bf16[1280,1152]{0,1:T(8,128)(2,1)} %bitcast.7), channel_id=1, source_target_pairs={{0,16},{1,17},{2,18},{3,19},{4,20},{5,21},{6,22},{7,23},{8,24},{9,... | collective-permute-start | bytes 8847368 | tf_op jit(solution)/shard_map/ppermute | solution.py:31
  23.0 71.9 %collective-permute-start = (bf16[1280,1152]{0,1:T(8,128)(2,1)}, bf16[1280,1152]{0,1:T(8,128)(2,1)}, u32[]{:S(2)}, u32[]{:S(2)}) collective-permute-start(bf16[1280,1152]{0,1:T(8,128)(2,1)} %bitcast.7), channel_id=1, source_target_pairs={{0,8},{1,9},{2,10},{3,11},{4,12},{5,13},{6,14},{7,15},{8,0},{9,1},... | collective-permute-start | bytes 8847368 | tf_op jit(solution)/shard_map/ppermute | solution.py:31
  31.7 187.3 %collective-permute-start.24 = (bf16[4,160,3,384]{3,1,2,0:T(8,128)(2,1)}, bf16[4,160,3,384]{3,1,2,0:T(8,128)(2,1)}, u32[]{:S(2)}, u32[]{:S(2)}) collective-permute-start(bf16[4,160,3,384]{3,1,2,0:T(8,128)(2,1)} %bitcast.204), channel_id=1, source_target_pairs={{0,1},{1,0},{2,3},{3,2},{4,5},{5,4},{6,7},{7,6},{8,9},{9,8},{10,11... | collective-permute-start | bytes 4423688 | tf_op jit(solution)/shard_map/ppermute | solution.py:31
  53.7 177.7 %collective-permute-start.25 = (bf16[4,160,1728]{2,1,0:T(8,128)(2,1)}, bf16[4,160,1728]{2,1,0:T(8,128)(2,1)}, u32[]{:S(2)}, u32[]{:S(2)}) collective-permute-start(bf16[4,160,1728]{2,1,0:T(8,128)(2,1)} %get-tuple-element.94), channel_id=1, source_target_pairs={{0,1},{1,0},{2,3},{3,2},{4,5},{5,4},{6,7},{7,6},{8,9},{9,8},{10,11... | collective-permute-start | bytes 6635528 | tf_op jit(solution)/shard_map/ppermute | solution.py:31
  56.5 151.9 %collective-permute-start.26 = (bf16[4,160,1728]{2,1,0:T(8,128)(2,1)}, bf16[4,160,1728]{2,1,0:T(8,128)(2,1)}, u32[]{:S(2)}, u32[]{:S(2)}) collective-permute-start(bf16[4,160,1728]{2,1,0:T(8,128)(2,1)} %get-tuple-element.92), channel_id=1, source_target_pairs={{0,1},{1,0},{2,3},{3,2},{4,5},{5,4},{6,7},{7,6},{8,9},{9,8},{10,11... | collective-permute-start | bytes 6635528 | tf_op jit(solution)/shard_map/ppermute | solution.py:31
  223.4 69.1 %collective-permute-start.44 = (bf16[80,3456]{1,0:T(8,128)(2,1)S(1)}, bf16[80,3456]{1,0:T(8,128)(2,1)}, u32[]{:S(2)}, u32[]{:S(2)}) collective-permute-start(bf16[80,3456]{1,0:T(8,128)(2,1)S(1)} %get-tuple-element.34), channel_id=1, source_target_pairs={{0,6},{1,7},{2,4},{3,5},{4,2},{5,3},{6,0},{7,1},{8,12},{9,13},{10,... | collective-permute-start | bytes 1658888 | tf_op jit(solution)/shard_map/ppermute | solution.py:31
  225.4 132.5 %collective-permute-start.42 = (bf16[80,3456]{1,0:T(8,128)(2,1)S(1)}, bf16[80,3456]{1,0:T(8,128)(2,1)S(1)}, u32[]{:S(2)}, u32[]{:S(2)}) collective-permute-start(bf16[80,3456]{1,0:T(8,128)(2,1)S(1)} %get-tuple-element.33), channel_id=1, source_target_pairs={{0,4},{1,5},{2,6},{3,7},{4,0},{5,1},{6,2},{7,3},{8,14},{9,15},{10,... | collective-permute-start | bytes 1658888 | tf_op jit(solution)/shard_map/ppermute | solution.py:31
  230.7 130.4 %collective-permute-start.28 = (bf16[80,3456]{1,0:T(8,128)(2,1)S(1)}, bf16[80,3456]{1,0:T(8,128)(2,1)S(1)}, u32[]{:S(2)}, u32[]{:S(2)}) collective-permute-start(bf16[80,3456]{1,0:T(8,128)(2,1)S(1)} %get-tuple-element.25), channel_id=1, source_target_pairs={{0,0},{1,1},{2,2},{3,3},{4,4},{5,5},{6,6},{7,7},{8,10},{9,11},{10,... | collective-permute-start | bytes 1658888 | tf_op jit(solution)/shard_map/ppermute | solution.py:31
  238.0 150.2 %collective-permute-start.40 = (bf16[80,3456]{1,0:T(8,128)(2,1)}, bf16[80,3456]{1,0:T(8,128)(2,1)}, u32[]{:S(2)}, u32[]{:S(2)}) collective-permute-start(bf16[80,3456]{1,0:T(8,128)(2,1)} %get-tuple-element.32), channel_id=1, source_target_pairs={{0,2},{1,3},{2,0},{3,1},{4,6},{5,7},{6,4},{7,5},{8,8},{9,9},{10,10... | collective-permute-start | bytes 1658888 | tf_op jit(solution)/shard_map/ppermute | solution.py:31
  241.2 153.2 %collective-permute-start.51 = (bf16[80,3456]{1,0:T(8,128)(2,1)}, bf16[80,3456]{1,0:T(8,128)(2,1)}, u32[]{:S(2)}, u32[]{:S(2)}) collective-permute-start(bf16[80,3456]{1,0:T(8,128)(2,1)} %get-tuple-element.37), channel_id=1, source_target_pairs={{0,6},{1,7},{2,4},{3,5},{4,2},{5,3},{6,0},{7,1},{8,12},{9,13},{10,... | collective-permute-start | bytes 1658888 | tf_op jit(solution)/shard_map/ppermute | solution.py:31
  292.5 128.6 %collective-permute-start.49 = (bf16[80,3456]{1,0:T(8,128)(2,1)}, bf16[80,3456]{1,0:T(8,128)(2,1)}, u32[]{:S(2)}, u32[]{:S(2)}) collective-permute-start(bf16[80,3456]{1,0:T(8,128)(2,1)} %get-tuple-element.36), channel_id=1, source_target_pairs={{0,4},{1,5},{2,6},{3,7},{4,0},{5,1},{6,2},{7,3},{8,14},{9,15},{10,... | collective-permute-start | bytes 1658888 | tf_op jit(solution)/shard_map/ppermute | solution.py:31
  437.6 122.7 %collective-permute-start.4 = (bf16[1280,768]{0,1:T(8,128)(2,1)S(1)}, bf16[1280,768]{0,1:T(8,128)(2,1)S(1)}, u32[]{:S(2)}, u32[]{:S(2)}) collective-permute-start(bf16[1280,768]{0,1:T(8,128)(2,1)S(1)} %copy-done.5), channel_id=1, source_target_pairs={{0,8},{1,9},{2,10},{3,11},{4,12},{5,13},{6,14},{7,15},{8,0},{9,1},... | collective-permute-start | bytes 5898248 | tf_op jit(solution)/shard_map/ppermute | solution.py:31
  439.5 126.6 %collective-permute-start.5 = (bf16[1280,768]{0,1:T(8,128)(2,1)S(1)}, bf16[1280,768]{0,1:T(8,128)(2,1)S(1)}, u32[]{:S(2)}, u32[]{:S(2)}) collective-permute-start(bf16[1280,768]{0,1:T(8,128)(2,1)S(1)} %copy-done.5), channel_id=1, source_target_pairs={{0,16},{1,17},{2,18},{3,19},{4,20},{5,21},{6,22},{7,23},{8,24},{9,... | collective-permute-start | bytes 5898248 | tf_op jit(solution)/shard_map/ppermute | solution.py:31
  461.1 84.8 %collective-permute-start.58 = (bf16[80,3456]{1,0:T(8,128)(2,1)S(1)}, bf16[80,3456]{1,0:T(8,128)(2,1)}, u32[]{:S(2)}, u32[]{:S(2)}) collective-permute-start(bf16[80,3456]{1,0:T(8,128)(2,1)S(1)} %copy-done.20), channel_id=1, source_target_pairs={{0,6},{1,7},{2,4},{3,5},{4,2},{5,3},{6,0},{7,1},{8,12},{9,13},{10,... | collective-permute-start | bytes 1658888 | tf_op jit(solution)/shard_map/ppermute | solution.py:31
  628.5 167.5 %collective-permute-start.37 = (bf16[160,2304]{1,0:T(8,128)(2,1)}, bf16[160,2304]{1,0:T(8,128)(2,1)}, u32[]{:S(2)}, u32[]{:S(2)}) collective-permute-start(bf16[160,2304]{1,0:T(8,128)(2,1)} %get-tuple-element.31), channel_id=1, source_target_pairs={{0,6},{1,7},{2,4},{3,5},{4,2},{5,3},{6,0},{7,1},{8,12},{9,13},{10,... | collective-permute-start | bytes 2211848 | tf_op jit(solution)/shard_map/ppermute | solution.py:31
  769.7 98.5 %collective-permute-start.21 = (bf16[1280,768]{1,0:T(8,128)(2,1)}, bf16[1280,768]{1,0:T(8,128)(2,1)}, u32[]{:S(2)}, u32[]{:S(2)}) collective-permute-start(bf16[1280,768]{1,0:T(8,128)(2,1)} %get-tuple-element.83), channel_id=1, source_target_pairs={{0,16},{1,17},{2,18},{3,19},{4,20},{5,21},{6,22},{7,23},{8,24},{9,... | collective-permute-start | bytes 5898248 | tf_op jit(solution)/shard_map/ppermute | solution.py:31
  772.1 98.4 %collective-permute-start.20 = (bf16[1280,768]{1,0:T(8,128)(2,1)}, bf16[1280,768]{1,0:T(8,128)(2,1)}, u32[]{:S(2)}, u32[]{:S(2)}) collective-permute-start(bf16[1280,768]{1,0:T(8,128)(2,1)} %get-tuple-element.84), channel_id=1, source_target_pairs={{0,8},{1,9},{2,10},{3,11},{4,12},{5,13},{6,14},{7,15},{8,0},{9,1},... | collective-permute-start | bytes 5898248 | tf_op jit(solution)/shard_map/ppermute | solution.py:31
  868.2 70.0 %collective-permute-start.32 = (bf16[160,2304]{1,0:T(8,128)(2,1)}, bf16[160,2304]{1,0:T(8,128)(2,1)}, u32[]{:S(2)}, u32[]{:S(2)}) collective-permute-start(bf16[160,2304]{1,0:T(8,128)(2,1)} %collective-permute-done.31), channel_id=1, source_target_pairs={{0,0},{1,1},{2,10},{3,11},{4,20},{5,21},{6,30},{7,31},{8,8},{9,9},... | collective-permute-start | bytes 2211848 | tf_op jit(solution)/shard_map/ppermute | solution.py:31
  870.6 83.3 %collective-permute-start.19 = (bf16[640,1280]{1,0:T(8,128)(2,1)}, bf16[640,1280]{1,0:T(8,128)(2,1)}, u32[]{:S(2)}, u32[]{:S(2)}) collective-permute-start(bf16[640,1280]{1,0:T(8,128)(2,1)} %bitcast.201), channel_id=1, source_target_pairs={{0,24},{1,25},{2,26},{3,27},{4,28},{5,29},{6,30},{7,31},{8,16},{9,... | collective-permute-start | bytes 4915208 | tf_op jit(solution)/shard_map/ppermute | solution.py:31
  883.9 88.9 %collective-permute-start.18 = (bf16[640,1280]{1,0:T(8,128)(2,1)}, bf16[640,1280]{1,0:T(8,128)(2,1)}, u32[]{:S(2)}, u32[]{:S(2)}) collective-permute-start(bf16[640,1280]{1,0:T(8,128)(2,1)} %bitcast.202), channel_id=1, source_target_pairs={{0,16},{1,17},{2,18},{3,19},{4,20},{5,21},{6,22},{7,23},{8,24},{9,... | collective-permute-start | bytes 4915208 | tf_op jit(solution)/shard_map/ppermute | solution.py:31
  885.9 86.9 %collective-permute-start.17 = (bf16[640,1280]{1,0:T(8,128)(2,1)}, bf16[640,1280]{1,0:T(8,128)(2,1)}, u32[]{:S(2)}, u32[]{:S(2)}) collective-permute-start(bf16[640,1280]{1,0:T(8,128)(2,1)} %bitcast.203), channel_id=1, source_target_pairs={{0,8},{1,9},{2,10},{3,11},{4,12},{5,13},{6,14},{7,15},{8,0},{9,1},... | collective-permute-start | bytes 4915208 | tf_op jit(solution)/shard_map/ppermute | solution.py:31
  888.2 110.0 %collective-permute-start.23 = (bf16[2048,768]{1,0:T(8,128)(2,1)}, bf16[2048,768]{1,0:T(8,128)(2,1)}, u32[]{:S(2)}, u32[]{:S(2)}) collective-permute-start(bf16[2048,768]{1,0:T(8,128)(2,1)} %get-tuple-element.76), channel_id=1, source_target_pairs={{0,1},{1,0},{2,3},{3,2},{4,5},{5,4},{6,7},{7,6},{8,9},{9,8},{10,11... | collective-permute-start | bytes 9437192 | tf_op jit(solution)/shard_map/ppermute | solution.py:31
  (81 other events, 2243.4 us)
Sparse Core Ops, SparseCore 0:
  15.2 120.3 all-gather.7
  194.1 232.3 all-gather.9
where the time goes:
time: 1040 us; the launch traced here: 1020 us
  waiting for transfers between devices  341 us (33%)
  starting transfers between devices  245 us (24%)
  local copies, waits for them, and re-layouts  205 us (20%)
  other arithmetic  75.7 us (7%)
  blocking collectives  54.7 us (5%)
  matrix products  43.2 us (4%)
  Pallas kernels  40.8 us (4%)
  between operations  19.8 us (2%)
    ppermute x67, waiting for transfers between devices, permute(): return lax.ppermute(x, BOTH, pairs)  305 us
    ppermute x67, starting transfers between devices, permute(): return lax.ppermute(x, BOTH, pairs)  244 us
    unnamed x81, local copies, waits for them, and re-layouts  41.7 us
    all_gather x1, waiting for transfers between devices, local(): gathered = lax.all_gather(quarter, 'col', axis=0, tiled=True)  36.7 us
    dynamic_slice x11, local copies, waits for them, and re-layouts, pick(): return lax.dynamic_index_in_dim(x, index, axis, keepdims=False)  36.4 us
    pallas_call x1, Pallas kernels, attend(): pl.pallas_call(kernel, grid_spec=pltpu.PrefetchScalarGridSpec(num_scalar_...  32.5 us
    all_gather x1, blocking collectives, local(): gain = pick(lax.all_gather(qk_gain, 'row', axis=0), plane)  32.3 us
    dot_general x4, matrix products, local(): jnp.dot(gathered[:, i * row_width:(i + 1) * row_width], weight_pieces[i],...  31.9 us
  transfers between devices with their start and end apart: 69, of which 16 were waited for; matrix products, arithmetic and copies ran while one was open for 29% of the time, Pallas kernels for 3%

commit v1 on v0

--- a/solution.py
+++ b/solution.py
@@ -31,8 +31,8 @@
     return lax.ppermute(x, BOTH, pairs)
 
 
-def after(x, *others):
-    return lax.optimization_barrier((x,) + others)[0]
+def together(*values):
+    return lax.optimization_barrier(values)
 
 
 def pick(x, index, axis=0):
@@ -69,11 +69,21 @@
         )
         return [x, first, second, third]
 
-    def across(self, block, i):
-        return self.move(block, lambda r, c: (r, (((c // 2) ^ i ^ r) * 2) + c % 2))
-
-    def down(self, block, i):
-        return self.move(block, lambda r, c: ((c // 2) ^ i ^ r, c))
+    def over_planes(self, blocks):
+        groups = [list(range(k, self.n_col, 2)) for k in range(2)]
+        return lax.all_to_all(
+            blocks, "col", split_axis=0, concat_axis=0, tiled=True, axis_index_groups=groups
+        )
+
+    def over_rows(self, blocks):
+        moved = [pick(blocks, self.row)]
+        for i in range(1, self.n_row):
+            moved.append(self.row_xor(pick(blocks, self.row ^ i), i))
+        return self.in_order(moved)
+
+    def in_order(self, moved):
+        stacked = jnp.stack(moved)
+        return [pick(stacked, r ^ self.row) for r in range(self.n_row)]
 
     def join_cores(self, mine, other, axis):
         return jnp.where(
@@ -165,30 +175,72 @@
     )(info, query, *kv_pieces)
 
 
-def page_kernel(info, pages_ref, out_ref):
+def turn_kernel(width, x_ref, scale_ref, angle_ref, gain_ref, query_ref, kv_ref):
+    cosine = angle_ref[:, :HD]
+    sine = angle_ref[:, HD:]
+    for j, (out_ref, base) in enumerate(((query_ref, 0), (kv_ref, 0))):
+        scale = scale_ref[:, j : j + 1]
+        for at in range(0, width, HD):
+            x = x_ref[:, j * width + at : j * width + at + HD]
+            x = x * scale * gain_ref[j : j + 1, at : at + HD]
+            turned = x * cosine + pltpu.roll(x, HD // 2, 1) * sine
+            out_ref[:, at : at + HD] = turned.astype(out_ref.dtype)
+    kv_ref[:, width:] = x_ref[:, 2 * width :].astype(kv_ref.dtype)
+
+
+def turn(projected, scales, angles, gain):
+    rows, width = projected.shape[0], projected.shape[1] // 3
+    step = 160 if rows % 160 == 0 else rows
+    return pl.pallas_call(
+        functools.partial(turn_kernel, width),
+        grid=(rows // step,),
+        in_specs=[
+            pl.BlockSpec((step, 3 * width), lambda b: (b, 0)),
+            pl.BlockSpec((step, 2), lambda b: (b, 0)),
+            pl.BlockSpec((step, 2 * HD), lambda b: (b, 0)),
+            pl.BlockSpec((2, width), lambda b: (0, 0)),
+        ],
+        out_specs=[
+            pl.BlockSpec((step, width), lambda b: (b, 0)),
+            pl.BlockSpec((step, 2 * width), lambda b: (b, 0)),
+        ],
+        out_shape=[
+            jax.ShapeDtypeStruct((rows, width), jnp.bfloat16),
+            jax.ShapeDtypeStruct((rows, 2 * width), jnp.bfloat16),
+        ],
+        cost_estimate=pl.CostEstimate(
+            flops=10 * rows * width, bytes_accessed=18 * rows * width, transcendentals=0
+        ),
+        name="turn",
+    )(projected, scales, angles, gain)
+
+
+def page_kernel(info, key_ref, value_ref, out_ref):
     page = info[pl.program_id(0)]
-    row = page * PAGE + lax.broadcasted_iota(jnp.int32, (1, PAGE, 1), 1)
+    row = page * PAGE + lax.broadcasted_iota(jnp.int32, (PAGE, 1), 0)
     inside = row < info[PAGES]
-    out_ref[0] = jnp.where(inside, pages_ref[0].astype(jnp.float32), 0.0).astype(out_ref.dtype)
-
-
-def place_pages(pages, info):
-    shape = pages.shape
-    spec = (1,) + shape[1:]
+    for j, ref in enumerate((key_ref, value_ref)):
+        kept = jnp.where(inside, ref[...].astype(jnp.float32), 0.0)
+        out_ref[0, j] = kept.astype(out_ref.dtype)
+
+
+def place_pages(keys, values, info):
+    width = keys.shape[1]
+    spec = pl.BlockSpec((PAGE, width), lambda s, info: (info[s], 0))
     return pl.pallas_call(
         page_kernel,
         grid_spec=pltpu.PrefetchScalarGridSpec(
             num_scalar_prefetch=1,
             grid=(PAGES,),
-            in_specs=[pl.BlockSpec(spec, lambda s, info: (info[s], 0, 0, 0))],
-            out_specs=pl.BlockSpec(spec, lambda s, info: (s, 0, 0, 0)),
+            in_specs=[spec, spec],
+            out_specs=pl.BlockSpec((1, 2, PAGE, width), lambda s, info: (s, 0, 0, 0)),
         ),
-        out_shape=jax.ShapeDtypeStruct(shape, pages.dtype),
+        out_shape=jax.ShapeDtypeStruct((PAGES, 2, PAGE, width), keys.dtype),
         cost_estimate=pl.CostEstimate(
-            flops=pages.size, bytes_accessed=4 * pages.size, transcendentals=0
+            flops=2 * keys.size, bytes_accessed=8 * keys.size, transcendentals=0
         ),
         name="place_pages",
-    )(info, pages)
+    )(info, keys, values)
 
 
 def local(
@@ -213,28 +265,60 @@
     quarter = lax.dynamic_slice_in_dim(hidden, row * part, part, 0).reshape(part, n_row, row_width)
     quarter = jnp.concatenate([pick(quarter, row ^ i, 1) for i in range(n_row)], axis=1)
     gathered = lax.all_gather(quarter, "col", axis=0, tiled=True)
+    gain = lax.all_gather(qk_gain, "row", axis=0)
     weights = qkv_train.astype(bf16).transpose(1, 0, 2).reshape(row_width, 3 * units)
+    weights, gain = together(weights, gain)
+    gain = pick(gain, plane)
     weight_pieces = grid.gather_row(weights)
-    gain = pick(lax.all_gather(qk_gain, "row", axis=0), plane)
+
+    def swap_cores(blocks, axis):
+        other = grid.other_core(pick(blocks, 1 - core, axis))
+        return pick(blocks, core, axis), other
+
+    qkv_blocks = grid.join_cores(
+        *swap_cores(weights.reshape(planes, 2, col_block, 3, units), 1), 3
+    ).reshape(planes, col_block, 6 * units)
+    ff = gate_up_train.astype(bf16).reshape(2, planes, 2, col_block, ff_units)
+    ff_blocks = grid.join_cores(*swap_cores(ff, 2), 3)
+    split = 2 if (col_block // 2) % 16 == 0 else 1
+    step_rows = col_block // split
+    chunks = [
+        ff_blocks[j, :, s * step_rows : (s + 1) * step_rows]
+        for j in range(2)
+        for s in range(split)
+    ]
+    at_planes = [grid.over_planes(chunks[0])]
+
+    head_rows = o_weight.shape[0] // 2
+    half_rows = lax.dynamic_slice_in_dim(o_weight, core * head_rows, head_rows, 0)
+    columns = [
+        lax.dynamic_slice_in_dim(half_rows, (row ^ i) * row_width, row_width, 1)
+        for i in range(n_row)
+    ]
+    all_weights, *columns = together(jnp.concatenate(weight_pieces, axis=0), *columns)
+    columns = [columns[0]] + [grid.row_xor(columns[i], i) for i in range(1, n_row)]
+    gathered, at_planes[0], qkv_blocks = together(gathered, at_planes[0], qkv_blocks)
+    at_planes_qkv = grid.over_planes(qkv_blocks)
+    at_rows = [grid.over_rows(at_planes[0])]
     whole_heads = units % HD == 0
     held = units if whole_heads else 2 * units
     if whole_heads:
         gain = lax.dynamic_slice_in_dim(gain, core * units, units, 1)
 
-    projected = 0.0
-    for i in range(n_row):
-        projected = projected + jnp.dot(
-            gathered[:, i * row_width : (i + 1) * row_width],
-            weight_pieces[i],
-            preferred_element_type=jnp.float32,
-        )
+    projected = jnp.dot(gathered, all_weights, preferred_element_type=jnp.float32)
     rows_here = n_col * part
-    projected = projected.reshape(rows_here, 3, units)
-    squares = jnp.sum(projected[:, :2] * projected[:, :2], axis=2)
-    squares = jnp.sum(lax.all_gather(squares.T, "col", axis=0), axis=0)
-    inverse = inverse_rms(squares, heads_width)
+    squares = jnp.stack(
+        [
+            jnp.sum(jnp.square(projected[:, j * units : (j + 1) * units]), axis=1)
+            for j in range(2)
+        ]
+    )
+    squares = jnp.sum(lax.all_gather(squares, "col", axis=0), axis=0)
+    inverse = inverse_rms(squares, heads_width).T
     if not whole_heads:
+        projected = projected.reshape(rows_here, 3, units)
         projected = grid.join_cores(projected, grid.other_core(projected), 2)
+        projected = projected.reshape(rows_here, 3 * held)
 
     token = (
         jnp.arange(n_col, dtype=jnp.int32)[:, None] * tokens
@@ -245,21 +329,27 @@
     position = token - start
     half = HD // 2
     frequency = rope_theta ** (-2.0 * jnp.arange(half, dtype=jnp.float32) / HD)
-    angles = position.astype(jnp.float32)[:, None] * frequency[None, :]
-    cosine = jnp.cos(angles)
-    sine = jnp.sin(angles)
-    cosine = jnp.concatenate([cosine, cosine], axis=1)[:, None, :]
-    sine = jnp.concatenate([-sine, sine], axis=1)[:, None, :]
-
-    def rotate(x):
-        x = x.reshape(rows_here, held // HD, HD)
-        swapped = jnp.concatenate([x[..., half:], x[..., :half]], axis=-1)
-        return (x * cosine + swapped * sine).reshape(rows_here, held).astype(bf16)
-
-    query = rotate(projected[:, 0] * inverse[0][:, None] * gain[0])
-    key = rotate(projected[:, 1] * inverse[1][:, None] * gain[1])
-    value = projected[:, 2].astype(bf16)
-    kv = jnp.concatenate([key, value], axis=1)
+    turns = position.astype(jnp.float32)[:, None] * frequency[None, :]
+    cosine, sine = jnp.cos(turns), jnp.sin(turns)
+    angles = jnp.concatenate([cosine, cosine, -sine, sine], axis=1)
+    query, kv = turn(projected, inverse, angles, gain)
+
+    query, kv, at_planes_qkv, chunks[1], at_rows[0], columns = together(
+        query, kv, at_planes_qkv, chunks[1], at_rows[0], columns
+    )
+    columns = jnp.stack(columns)
+    columns_other = grid.other_core(columns)
+    at_planes.append(grid.over_planes(chunks[1]))
+    key_or_value = [
+        lax.dynamic_slice_in_dim(kv, j * held + core * units, units, 1)
+        if not whole_heads
+        else kv[:, j * units : (j + 1) * units]
+        for j in range(2)
+    ]
+    same_core = [list(range(k, n_col, 2)) for k in range(2)]
+    key_planes, value_planes = [
+        lax.all_gather(x, "col", axis=0, axis_index_groups=same_core) for x in key_or_value
+    ]
 
     kv_pieces = [x.reshape(n_col, part, 2 * held) for x in grid.gather_row(kv)]
     offsets = jnp.stack([(row ^ i) * part for i in range(n_row)])
@@ -269,7 +359,23 @@
         kv_pieces = [natural.reshape(n_col, tokens, 2 * held)]
         offsets = jnp.zeros((1,), jnp.int32)
     info = jnp.concatenate([prompt_ends, (row * part)[None], offsets]).astype(jnp.int32)
+    kv_pieces[-1], at_planes_qkv = together(kv_pieces[-1], at_planes_qkv)
+    at_rows_qkv = grid.over_rows(at_planes_qkv)
     attention = attend(query.reshape(n_col, part, held), kv_pieces, info, tokens, prompts)
+
+    attention, at_planes[1], key_planes, at_rows_qkv, columns_other = together(
+        attention, at_planes[1], key_planes, at_rows_qkv, columns_other
+    )
+    at_rows.append(grid.over_rows(at_planes[1]))
+    key_rows = lax.all_to_all(key_planes, "row", split_axis=0, concat_axis=0, tiled=True)
+
+    def place_rows(whole, first, parts):
+        for at, blocks in enumerate(parts, first):
+            j, s = divmod(at, split)
+            whole = lax.dynamic_update_slice(
+                whole, jnp.stack(blocks)[None], (j, 0, s * step_rows, 0)
+            )
+        return whole
 
     attention = attention.reshape(planes, 2, part, held)
     mine = pick(attention, core, 1)
@@ -278,49 +384,57 @@
     else:
         attention = mine
     arrived = jnp.stack(
+        [pick(attention, plane)]
+        + [
+            grid.move(pick(attention, plane ^ i), lambda r, c: (r, c ^ (2 * i)))
+            for i in range(1, planes)
+        ]
+    )
+    arrived, key_rows, chunks[2:3], at_rows[1], value_planes = together(
+        arrived, key_rows, chunks[2:3], at_rows[1], value_planes
+    )
+    at_planes += [grid.over_planes(chunk) for chunk in chunks[2:3]]
+    o_columns = jnp.concatenate(
         [
-            grid.down(grid.across(pick(attention, plane ^ i ^ row), i), i)
-            for i in range(n_row)
-        ]
-    )
-    attention_rows = jnp.concatenate(
-        [pick(arrived, r ^ row ^ plane) for r in range(n_row)], axis=0
-    )
-    partial_out = jnp.dot(attention_rows, o_weight, preferred_element_type=jnp.float32).astype(bf16)
-    partial_out = partial_out.reshape(tokens, n_row, row_width)
-    summed = pick(partial_out, row, 1).astype(jnp.float32)
-    for i in range(1, n_row):
-        summed = summed + grid.row_xor(pick(partial_out, row ^ i, 1), i).astype(jnp.float32)
+            grid.join_cores(pick(columns, row ^ r), pick(columns_other, row ^ r), 0)
+            for r in range(n_row)
+        ],
+        axis=0,
+    )
+    ff_server = jnp.zeros((2, n_row, col_block, 2 * ff_units), bf16)
+    ff_server = place_rows(ff_server, 0, at_rows)
+    attention = jnp.concatenate([pick(arrived, h ^ plane) for h in range(planes)], axis=1)
+    attention_rows = jnp.concatenate(grid.in_order(grid.gather_row(attention)), axis=0)
+    attention_rows, at_planes[2:], chunks[3:] = together(
+        attention_rows, at_planes[2:], chunks[3:]
+    )
+    at_rows += [grid.over_rows(blocks) for blocks in at_planes[2:]]
+    at_planes += [grid.over_planes(chunk) for chunk in chunks[3:]]
+    value_rows = jnp.stack(grid.over_rows(value_planes))
+    summed = jnp.dot(attention_rows, o_columns, preferred_element_type=jnp.float32)
     out_squares = lax.psum(jnp.sum(summed * summed, axis=1), "row")
     normalized = summed * inverse_rms(out_squares, width)[:, None] * post_gain
     residual = lax.dynamic_slice_in_dim(hidden, row * row_width, row_width, 1).astype(jnp.float32)
     layer_out = (residual + normalized).astype(bf16)
-
-    if not whole_heads:
-        kv = jnp.concatenate(
-            [lax.dynamic_slice_in_dim(x, core * units, units, 1) for x in (key, value)], axis=1
-        )
-    same_core = [list(range(k, n_col, 2)) for k in range(2)]
-    kv_planes = lax.all_gather(kv, "col", axis=0, axis_index_groups=same_core)
-    cache_pieces = [pick(kv_planes, row)] + [
-        grid.row_xor(pick(kv_planes, row ^ i), i) for i in range(1, n_row)
-    ]
-    stacked = jnp.stack(cache_pieces).reshape(n_row, n_col, part, 2 * units)
-    natural = jnp.stack([pick(stacked, row ^ r) for r in range(n_row)], axis=1)
-    natural = natural.reshape(n_col * tokens, 2 * units)
+    ff_server = place_rows(ff_server, 2, at_rows[2:])
+    layer_out, at_planes[3:], ff_server = together(layer_out, at_planes[3:], ff_server)
+    at_rows += [grid.over_rows(blocks) for blocks in at_planes[3:]]
+    ff_server = place_rows(ff_server, 3, at_rows[3:])
+
     most = PAGES * PAGE
-    natural = jnp.concatenate([natural, jnp.zeros((most, 2 * units), bf16)], axis=0)
 
     def start_of(owner_col):
         return jnp.sum(jnp.where(owner == owner_col, prompt_starts, 0))
 
-    window_other = grid.other_core(
-        lax.dynamic_slice_in_dim(natural, start_of(col ^ 1), most, 0)
-    )
-    window = lax.dynamic_slice_in_dim(natural, start_of(col), most, 0)
-    pages = grid.join_cores(
-        window.reshape(PAGES, PAGE, 2, units), window_other.reshape(PAGES, PAGE, 2, units), 3
-    ).transpose(0, 2, 1, 3)
+    def window(rows):
+        rows = rows.reshape(n_row, n_col, part, units).transpose(1, 0, 2, 3)
+        rows = rows.reshape(n_col * tokens, units)
+        rows = jnp.concatenate([rows, jnp.zeros((most, units), bf16)], axis=0)
+        other = grid.other_core(lax.dynamic_slice_in_dim(rows, start_of(col ^ 1), most, 0))
+        return grid.join_cores(
+            lax.dynamic_slice_in_dim(rows, start_of(col), most, 0), other, 1
+        )
+
     mine = owner == col
     my_length = jnp.sum(jnp.where(mine, lengths, 0))
     my_table = jnp.sum(jnp.where(mine[:, None], page_table, 0), axis=0)
@@ -329,44 +443,14 @@
         jnp.where(my_table[None, :] == page_index[:, None], page_index[None, :], 0), axis=1
     )
     page_of_slot = jnp.where(jnp.any(mine), page_of_slot, 0)
-    cache = place_pages(pages, jnp.concatenate([page_of_slot, my_length[None]]).astype(jnp.int32))
-
-    def swap_cores(blocks):
-        other = grid.other_core(pick(blocks, 1 - core, 1))
-        return pick(blocks, core, 1), other
-
-    qkv_mine, qkv_other = swap_cores(weights.reshape(planes, 2, col_block, 3, units))
-    qkv_blocks = grid.join_cores(qkv_mine, qkv_other, 3).reshape(planes, col_block, 6 * units)
-    ff = gate_up_train.astype(bf16).reshape(2, planes, 2, col_block, ff_units)
-    ff_blocks = [grid.join_cores(*swap_cores(ff[j]), 2) for j in range(2)]
-
-    split = 2 if (col_block // 2) % 16 == 0 else 1
-    step_rows = col_block // split
-    chunks = [(b, s * step_rows) for b in ff_blocks for s in range(split)]
-    chunks.append((qkv_blocks, None))
-    results = []
-    gate = gathered
-    for blocks, at in chunks:
-        sent = []
-        for i in range(n_row):
-            block = pick(blocks, plane ^ i ^ row)
-            if at is not None:
-                block = block[at : at + step_rows]
-            sent.append(grid.across(after(block, gate), i))
-        gate = sent[0][:8, :128]
-        results.append(
-            jnp.stack([grid.down(x, i) for i, x in enumerate(sent)])
-        )
-
-    def in_order(rounds):
-        return jnp.stack([pick(rounds, r ^ row ^ plane) for r in range(n_row)])
-
-    qkv_server = in_order(results[-1]).reshape(n_row, col_block, 3, 2 * units).transpose(2, 0, 1, 3)
-    ff_server = [
-        jnp.concatenate([in_order(x) for x in results[j * split : (j + 1) * split]], axis=1)
-        for j in range(2)
-    ]
-    return (layer_out, cache[None], qkv_server, jnp.stack(ff_server))
+    cache = place_pages(
+        window(key_rows),
+        window(value_rows),
+        jnp.concatenate([page_of_slot, my_length[None]]).astype(jnp.int32),
+    )
+
+    qkv_server = jnp.stack(at_rows_qkv).reshape(n_row, col_block, 3, 2 * units).transpose(2, 0, 1, 3)
+    return (layer_out, cache[None], qkv_server, ff_server)
 
 
 def solution(mesh):

time: 1040 us -> 705 us (0.68)
  the two profiles are of different devices: /device:TPU:16 before, /device:TPU:0 now
where the time goes in v1:
time: 705 us; the launch traced here: 699 us
  waiting for transfers between devices  232 us (33%)
  local copies, waits for them, and re-layouts  152 us (22%)
  other arithmetic  77.4 us (11%)
  starting transfers between devices  70.7 us (10%)
  blocking collectives  66.7 us (9%)
  Pallas kernels  53.1 us (8%)
  matrix products  28 us (4%)
  between operations  18.6 us (3%)
    ppermute x42, waiting for transfers between devices, permute(): return lax.ppermute(x, BOTH, pairs)  185 us
    ppermute x42, starting transfers between devices, permute(): return lax.ppermute(x, BOTH, pairs)  42.9 us
    all_gather x1, blocking collectives, local(): squares = jnp.sum(lax.all_gather(squares, 'col', axis=0), axis=0)  38.4 us
    pallas_call x1, Pallas kernels, attend(): pl.pallas_call(kernel, grid_spec=pltpu.PrefetchScalarGridSpec(num_scalar_...  33 us
    unnamed x65, local copies, waits for them, and re-layouts  32.3 us
    select_n x8, other arithmetic, join_cores(): jnp.where(self.core == 0, jnp.concatenate([mine, other], axis=axis), jnp....  30.9 us
    all_to_all x5, waiting for transfers between devices, over_planes(): lax.all_to_all(blocks, 'col', split_axis=0, concat_axis=0, tiled=True, ax...  30.2 us
    dynamic_slice x14, local copies, waits for them, and re-layouts, pick(): return lax.dynamic_index_in_dim(x, index, axis, keepdims=False)  28.8 us
  transfers between devices with their start and end apart: 51, of which 22 were waited for; matrix products, arithmetic and copies ran while one was open for 34% of the time, Pallas kernels for 8%

profile of v1, /device:TPU:0, one launch (start us, length us, event | category | flops | bytes accessed | tf_op | source)
XLA Modules:
  0.0 698.5 jit_solution(6229333825850491728)
XLA Ops:
  15.1 15.8 %copy.74 = bf16[2,1280,1728]{2,1,0:T(8,128)(2,1)} copy(f32[2,1280,1728]{1,2,0:T(8,128)} %param.17) | data formatting | bytes 26542080 | tf_op args[8]
  30.9 8.0 %dynamic-slice_bitcast_fusion.1 = (bf16[2,4,160,1728]{3,2,1,0:T(8,128)(2,1)}, bf16[2,4,160,1728]{3,2,1,0:T(8,128)(2,1)}) fusion(bf16[2,4,2,160,1728]{4,3,2,1,0:T(8,128)(2,1)} %bitcast.228, s32[]{:T(128)S(6)} %select_n.262, s32[]{:T(128)S(6)} %select_n.263), kind=kLoop, calls=%fused_computation.14 | loop fusion | bytes 17694728 | tf_op jit(solution)/shard_map/jit(dynamic_index_in_dim)/squeeze | solution.py:39
  44.2 9.5 %all-gather.4 = f32[4,2,768]{2,1,0:T(2,128)S(1)} all-gather(f32[1,2,768]{2,1,0:T(2,128)S(1)} %bitcast.261), channel_id=2, replica_groups=mesh['row'=4,'col'=8] {'row'}, dimensions={0}, use_global_device_ids=true | all-gather | bytes 30720 | tf_op jit(solution)/shard_map/all_gather | solution.py:268
  59.1 7.3 %reshape.136 = bf16[4,2,160,3,384]{4,3,2,1,0:T(4,128)(2,1)} reshape(bf16[1280,1152]{1,0:T(8,128)(2,1)} %copy.76) | data formatting | bytes 5898240 | tf_op jit(solution)/shard_map/reshape | solution.py:279
  79.9 13.5 %maximum_select_fusion = bf16[2,4,160,3456]{3,2,1,0:T(8,128)(2,1)S(1)} fusion(bf16[2,4,160,1728]{3,2,1,0:T(8,128)(2,1)} %collective-permute-done, bf16[2,4,160,1728]{3,2,1,0:T(8,128)(2,1)} %get-tuple-element.135, pred[]{:T(512)S(6)} %eq.18), kind=kLoop, calls=%fused_computation | loop fusion | flops 39813120 | bytes 17694720 | tf_op jit(solution)/shard_map/jit(_where)/select_n | solution.py:89
  109.7 9.1 %collective-permute-done.2 = bf16[1280,1152]{0,1:T(8,128)(2,1)} collective-permute-done((bf16[1280,1152]{0,1:T(8,128)(2,1)S(1)}, bf16[1280,1152]{0,1:T(8,128)(2,1)}, u32[]{:S(2)}, u32[]{:S(2)}) %collective-permute-start.2) | collective-permute-done | bytes 2949152 | tf_op jit(solution)/shard_map/ppermute | solution.py:31
  132.8 20.0 %collective-permute-done.4 = bf16[640,1152]{0,1:T(8,128)(2,1)S(1)} collective-permute-done((bf16[640,1152]{0,1:T(8,128)(2,1)S(1)}, bf16[640,1152]{0,1:T(8,128)(2,1)S(1)}, u32[]{:S(2)}, u32[]{:S(2)}) %collective-permute-start.4) | collective-permute-done | bytes 1474592 | tf_op jit(solution)/shard_map/ppermute | solution.py:31
  166.6 18.0 %all-to-all-done = bf16[4,80,3456]{2,1,0:T(8,128)(2,1)} async-done(((bf16[4,80,3456]{2,1,0:T(8,128)(2,1)}), bf16[4,80,3456]{2,1,0:T(8,128)(2,1)}, u32[]{:S(2)}, u32[]{:S(2)}) %all-to-all-start) | async-done | bytes 2211872 | tf_op jit(solution)/shard_map/all_to_all | solution.py:74
  189.3 19.2 %fusion.22 = f32[1280,1152]{0,1:T(8,128)S(1)} fusion(bf16[1280,5120]{1,0:T(8,128)(2,1)} %all-gather.10.cloned.1.call-done, bf16[5120,1152]{0,1:T(8,128)(2,1)} %copy-done.22), kind=kOutput, calls=%fused_computation.174 | convolution fusion | flops 15099494400 | bytes 30801920 | tf_op jit(solution)/shard_map/dot_general | solution.py:308
  216.5 7.7 %copy.82.x_ref = f32[1280,1152]{1,0:T(8,128)} copy(f32[1280,1152]{0,1:T(8,128)} %copy-done.2) | data formatting | bytes 11796480 | tf_op jit(solution)/shard_map/dot_general | solution.py:308
  224.1 38.4 %all-gather.5 = f32[8,2,1280]{2,1,0:T(2,128)S(1)} all-gather(f32[1,2,1280]{2,1,0:T(2,128)S(1)} %maximum_bitcast_fusion.6), channel_id=3, replica_groups=mesh['row'=4,'col'=8] {'col'}, dimensions={0}, use_global_device_ids=true | all-gather | bytes 92160 | tf_op jit(solution)/shard_map/all_gather | solution.py:316
  263.7 7.9 %turn.1 = (bf16[1280,384]{1,0:T(8,128)(2,1)}, bf16[1280,768]{1,0:T(8,128)(2,1)}) custom-call(f32[1280,1152]{1,0:T(8,128)} %copy.82.x_ref, f32[1280,2]{1,0:T(8,128)} %bitcast.241, f32[1280,256]{1,0:T(8,128)} %pad_maximum_fusion.12.angle_ref, f32[2,384]{1,0:T(2,128)} %fusion.15.gain_ref), custom_call_target="tpu_custom_call" | custom-call | flops 4915200 | bytes 8847360 | tf_op jit(solution)/shard_map/turn/pallas_call | solution.py:194
  275.6 21.2 %collective-permute-done.11 = bf16[384,1280]{1,0:T(8,128)(2,1)} collective-permute-done((bf16[384,1280]{1,0:T(8,128)(2,1)}, bf16[384,1280]{1,0:T(8,128)(2,1)}, u32[]{:S(2)}, u32[]{:S(2)}) %collective-permute-start.11) | collective-permute-done | bytes 983072 | tf_op jit(solution)/shard_map/ppermute | solution.py:31
  310.5 32.2 %collective-permute-done.13 = bf16[1280,768]{1,0:T(8,128)(2,1)} collective-permute-done((bf16[1280,768]{1,0:T(8,128)(2,1)S(1)}, bf16[1280,768]{1,0:T(8,128)(2,1)}, u32[]{:S(2)}, u32[]{:S(2)}) %collective-permute-start.13) | collective-permute-done | bytes 1966112 | tf_op jit(solution)/shard_map/ppermute | solution.py:31
  383.5 33.0 %attend.1 = bf16[8,160,384]{2,1,0:T(8,128)(2,1)S(1)} custom-call(s32[9]{0:T(128)S(1)} %concatenate.91.info, bf16[8,160,384]{2,1,0:T(8,128)(2,1)S(1)} %bitcast.227, bf16[8,160,768]{2,1,0:T(8,128)(2,1)S(1)} %bitcast.225, bf16[8,160,768]{2,1,0:T(8,128)(2,1)} %bitcast.31.refs_1_, bf16[8,160,768]{2,1,0:T(8,128)(2,1)} %bitcast.32.refs_2_, ...), custom_call_target="tpu_custom_call" | custom-call | flops 3774873600 | bytes 9830400 | tf_op jit(solution)/shard_map/attend/pallas_call | solution.py:158
  458.2 28.3 %collective-permute-done.26 = bf16[80,3456]{1,0:T(8,128)(2,1)} collective-permute-done((bf16[80,3456]{1,0:T(8,128)(2,1)}, bf16[80,3456]{1,0:T(8,128)(2,1)}, u32[]{:S(2)}, u32[]{:S(2)}) %collective-permute-start.26) | collective-permute-done | bytes 552992 | tf_op jit(solution)/shard_map/ppermute | solution.py:31
  486.5 10.5 %collective-permute-done.25 = bf16[80,3456]{1,0:T(8,128)(2,1)} collective-permute-done((bf16[80,3456]{1,0:T(8,128)(2,1)}, bf16[80,3456]{1,0:T(8,128)(2,1)}, u32[]{:S(2)}, u32[]{:S(2)}) %collective-permute-start.25) | collective-permute-done | bytes 552992 | tf_op jit(solution)/shard_map/ppermute | solution.py:31
  505.8 13.4 %all-gather.14.cloned.1.call-done = bf16[5120,384]{1,0:T(8,128)(2,1)} async-done(((bf16[1280,384]{1,0:T(8,128)(2,1)}), bf16[5120,384]{1,0:T(8,128)(2,1)}) %all-gather.14.cloned.1.call-update) | async-done | bytes 3932176 | tf_op jit(solution)/shard_map/all_gather | solution.py:351
  550.5 17.5 %collective-permute-done.37 = bf16[1280,384]{1,0:T(8,128)(2,1)} collective-permute-done((bf16[1280,384]{1,0:T(8,128)(2,1)}, bf16[1280,384]{1,0:T(8,128)(2,1)}, u32[]{:S(2)}, u32[]{:S(2)}) %collective-permute-start.37) | collective-permute-done | bytes 983072 | tf_op jit(solution)/shard_map/ppermute | solution.py:31
  569.5 18.0 %collective-permute-done.36 = bf16[1280,384]{1,0:T(8,128)(2,1)} collective-permute-done((bf16[1280,384]{1,0:T(8,128)(2,1)}, bf16[1280,384]{1,0:T(8,128)(2,1)}, u32[]{:S(2)}, u32[]{:S(2)}) %collective-permute-start.36) | collective-permute-done | bytes 983072 | tf_op jit(solution)/shard_map/ppermute | solution.py:31
  611.9 8.8 %multiply_reduce_fusion = (f32[640]{0:T(1024)S(1)}, f32[640,1280]{1,0:T(8,128)S(1)}) fusion(bf16[640,3072]{1,0:T(8,128)(2,1)S(1)} %copy-done.7, bf16[768,1280]{1,0:T(8,128)(2,1)} %maximum_select_fusion.7, bf16[768,1280]{1,0:T(8,128)(2,1)} %maximum_select_fusion.6, bf16[768,1280]{1,0:T(8,128)(2,1)} %maximum_select_fusion.5, ...), kind=kOutput, calls=%fused_computation.22 | convolution fusion | flops 5066259968 | bytes 15075840 | tf_op jit(solution)/shard_map/dot_general | solution.py:414
  620.7 18.8 %psum.7 = f32[640]{0:T(1024)S(1)} all-reduce(f32[640]{0:T(1024)S(1)} %get-tuple-element.232), channel_id=1, replica_groups=mesh['row'=4,'col'=8] {'row'}, use_global_device_ids=true, to_apply=%region_6.7 | all-reduce | flops 640 | bytes 5120 | tf_op jit(solution)/shard_map/psum | solution.py:415
  646.4 12.1 %all-to-all-done.5 = bf16[4,80,3456]{2,1,0:T(8,128)(2,1)} async-done(((bf16[4,80,3456]{2,1,0:T(8,128)(2,1)}), bf16[4,80,3456]{2,1,0:T(8,128)(2,1)}, u32[]{:S(2)}, u32[]{:S(2)}) %all-to-all-start.5) | async-done | bytes 2211872 | tf_op jit(solution)/shard_map/all_to_all | solution.py:74
  672.5 12.3 %place_pages.1 = bf16[16,2,128,768]{3,2,1,0:T(8,128)(2,1)} custom-call(s32[17]{0:T(128)} %pad_add_fusion.info, bf16[2048,768]{1,0:T(8,128)(2,1)} %maximum_select_fusion.1.key_ref, bf16[2048,768]{1,0:T(8,128)(2,1)} %maximum_select_fusion.2.value_ref), custom_call_target="tpu_custom_call" | custom-call | flops 3145728 | bytes 12582912 | tf_op jit(solution)/shard_map/place_pages/pallas_call | solution.py:230
  (257 shorter events, 279.3 us)
Async XLA Ops:
  7.2 177.5 %all-gather.10.cloned.1.call-start = ((), (), s32[]{:S(2)}) async-start(), calls=%async_computation.6 | async-start | bytes 14745600 | tf_op jit(solution)/shard_map/all_gather | solution.py:267
  53.7 65.1 %collective-permute-start.2 = (bf16[1280,1152]{0,1:T(8,128)(2,1)S(1)}, bf16[1280,1152]{0,1:T(8,128)(2,1)}, u32[]{:S(2)}, u32[]{:S(2)}) collective-permute-start(bf16[1280,1152]{0,1:T(8,128)(2,1)S(1)} %bitcast.229), channel_id=1, source_target_pairs={{0,8},{1,9},{2,10},{3,11},{4,12},{5,13},{6,14},{7,15},{8,0},{9,1},... | collective-permute-start | bytes 8847368 | tf_op jit(solution)/shard_map/ppermute | solution.py:31
  55.2 71.0 %collective-permute-start.3 = (bf16[1280,1152]{0,1:T(8,128)(2,1)S(1)}, bf16[1280,1152]{0,1:T(8,128)(2,1)}, u32[]{:S(2)}, u32[]{:S(2)}) collective-permute-start(bf16[1280,1152]{0,1:T(8,128)(2,1)S(1)} %bitcast.230), channel_id=1, source_target_pairs={{0,16},{1,17},{2,18},{3,19},{4,20},{5,21},{6,22},{7,23},{8,24},{9,... | collective-permute-start | bytes 8847368 | tf_op jit(solution)/shard_map/ppermute | solution.py:31
  97.0 87.6 %all-to-all-start = ((bf16[4,80,3456]{2,1,0:T(8,128)(2,1)}), bf16[4,80,3456]{2,1,0:T(8,128)(2,1)}, u32[]{:S(2)}, u32[]{:S(2)}) async-start(bf16[4,80,3456]{2,1,0:T(8,128)(2,1)} %get-tuple-element.140), calls=%async_computation | async-start | bytes 4423680 | tf_op jit(solution)/shard_map/all_to_all | solution.py:74
  164.6 111.0 %collective-permute-start.9 = (bf16[384,1280]{1,0:T(8,128)(2,1)}, bf16[384,1280]{1,0:T(8,128)(2,1)}, u32[]{:S(2)}, u32[]{:S(2)}) collective-permute-start(bf16[384,1280]{1,0:T(8,128)(2,1)} %get-tuple-element.61), channel_id=1, source_target_pairs={{0,8},{1,9},{2,10},{3,11},{4,12},{5,13},{6,14},{7,15},{8,0},{9,1},... | collective-permute-start | bytes 2949128 | tf_op jit(solution)/shard_map/ppermute | solution.py:31
  165.1 110.5 %collective-permute-start.10 = (bf16[384,1280]{1,0:T(8,128)(2,1)}, bf16[384,1280]{1,0:T(8,128)(2,1)}, u32[]{:S(2)}, u32[]{:S(2)}) collective-permute-start(bf16[384,1280]{1,0:T(8,128)(2,1)} %get-tuple-element.62), channel_id=1, source_target_pairs={{0,16},{1,17},{2,18},{3,19},{4,20},{5,21},{6,22},{7,23},{8,24},{9,... | collective-permute-start | bytes 2949128 | tf_op jit(solution)/shard_map/ppermute | solution.py:31
  184.6 112.2 %all-to-all-start.1 = ((bf16[4,160,2304]{2,1,0:T(8,128)(2,1)}), bf16[4,160,2304]{2,1,0:T(8,128)(2,1)}, u32[]{:S(2)}, u32[]{:S(2)}) async-start(bf16[4,160,2304]{2,1,0:T(8,128)(2,1)} %bitcast.138), calls=%async_computation.1 | async-start | bytes 5898240 | tf_op jit(solution)/shard_map/all_to_all | solution.py:74
  189.2 232.7 %all-gather.12.cloned.1.call-start = ((), (), s32[]{:S(2)}) async-start(), calls=%async_computation.7 | async-start | bytes 4915200 | tf_op jit(solution)/shard_map/all_gather | solution.py:351
  213.0 58.6 %collective-permute-start.8 = (bf16[80,3456]{1,0:T(8,128)(2,1)}, bf16[80,3456]{1,0:T(8,128)(2,1)S(1)}, u32[]{:S(2)}, u32[]{:S(2)}) collective-permute-start(bf16[80,3456]{1,0:T(8,128)(2,1)} %get-tuple-element.208), channel_id=1, source_target_pairs={{0,24},{1,25},{2,26},{3,27},{4,28},{5,29},{6,30},{7,31},{8,16},{9,... | collective-permute-start | bytes 1658888 | tf_op jit(solution)/shard_map/ppermute | solution.py:31
  215.3 58.7 %collective-permute-start.7 = (bf16[80,3456]{1,0:T(8,128)(2,1)S(1)}, bf16[80,3456]{1,0:T(8,128)(2,1)S(1)}, u32[]{:S(2)}, u32[]{:S(2)}) collective-permute-start(bf16[80,3456]{1,0:T(8,128)(2,1)S(1)} %get-tuple-element.209), channel_id=1, source_target_pairs={{0,16},{1,17},{2,18},{3,19},{4,20},{5,21},{6,22},{7,23},{8,24},{9,... | collective-permute-start | bytes 1658888 | tf_op jit(solution)/shard_map/ppermute | solution.py:31
  215.9 58.1 %collective-permute-start.6 = (bf16[80,3456]{1,0:T(8,128)(2,1)S(1)}, bf16[80,3456]{1,0:T(8,128)(2,1)S(1)}, u32[]{:S(2)}, u32[]{:S(2)}) collective-permute-start(bf16[80,3456]{1,0:T(8,128)(2,1)S(1)} %get-tuple-element.210), channel_id=1, source_target_pairs={{0,8},{1,9},{2,10},{3,11},{4,12},{5,13},{6,14},{7,15},{8,0},{9,1},... | collective-permute-start | bytes 1658888 | tf_op jit(solution)/shard_map/ppermute | solution.py:31
  304.9 113.5 %collective-permute-start.19 = (bf16[4,384,1280]{2,1,0:T(8,128)(2,1)}, bf16[4,384,1280]{2,1,0:T(8,128)(2,1)}, u32[]{:S(2)}, u32[]{:S(2)}) collective-permute-start(bf16[4,384,1280]{2,1,0:T(8,128)(2,1)} %pad_maximum_fusion), channel_id=1, source_target_pairs={{0,1},{1,0},{2,3},{3,2},{4,5},{5,4},{6,7},{7,6},{8,9},{9,8},{10,11... | collective-permute-start | bytes 11796488 | tf_op jit(solution)/shard_map/ppermute | solution.py:31
  305.7 112.7 %all-to-all-start.2 = ((bf16[4,80,3456]{2,1,0:T(8,128)(2,1)}), bf16[4,80,3456]{2,1,0:T(8,128)(2,1)}, u32[]{:S(2)}, u32[]{:S(2)}) async-start(bf16[4,80,3456]{2,1,0:T(8,128)(2,1)} %get-tuple-element.68), calls=%async_computation.2 | async-start | bytes 4423680 | tf_op jit(solution)/shard_map/all_to_all | solution.py:74
  310.3 208.9 %all-gather.14.cloned.1.call-start = ((), (), s32[]{:S(2)}) async-start(), calls=%async_computation.8 | async-start | bytes 4915200 | tf_op jit(solution)/shard_map/all_gather | solution.py:351
  423.0 96.2 %all-to-all-start.3 = ((bf16[4,1280,384]{2,1,0:T(8,128)(2,1)}), bf16[4,1280,384]{2,1,0:T(8,128)(2,1)}, u32[]{:S(2)}, u32[]{:S(2)}) async-start(bf16[4,1280,384]{2,1,0:T(8,128)(2,1)} %bitcast.238), calls=%async_computation.3 | async-start | bytes 7864320 | tf_op jit(solution)/shard_map/all_to_all | solution.py:370
  430.9 55.7 %collective-permute-start.26 = (bf16[80,3456]{1,0:T(8,128)(2,1)}, bf16[80,3456]{1,0:T(8,128)(2,1)}, u32[]{:S(2)}, u32[]{:S(2)}) collective-permute-start(bf16[80,3456]{1,0:T(8,128)(2,1)} %get-tuple-element.200), channel_id=1, source_target_pairs={{0,24},{1,25},{2,26},{3,27},{4,28},{5,29},{6,30},{7,31},{8,16},{9,... | collective-permute-start | bytes 1658888 | tf_op jit(solution)/shard_map/ppermute | solution.py:31
  433.7 63.3 %collective-permute-start.25 = (bf16[80,3456]{1,0:T(8,128)(2,1)}, bf16[80,3456]{1,0:T(8,128)(2,1)}, u32[]{:S(2)}, u32[]{:S(2)}) collective-permute-start(bf16[80,3456]{1,0:T(8,128)(2,1)} %get-tuple-element.201), channel_id=1, source_target_pairs={{0,16},{1,17},{2,18},{3,19},{4,20},{5,21},{6,22},{7,23},{8,24},{9,... | collective-permute-start | bytes 1658888 | tf_op jit(solution)/shard_map/ppermute | solution.py:31
  434.3 62.8 %collective-permute-start.24 = (bf16[80,3456]{1,0:T(8,128)(2,1)}, bf16[80,3456]{1,0:T(8,128)(2,1)}, u32[]{:S(2)}, u32[]{:S(2)}) collective-permute-start(bf16[80,3456]{1,0:T(8,128)(2,1)} %get-tuple-element.202), channel_id=1, source_target_pairs={{0,8},{1,9},{2,10},{3,11},{4,12},{5,13},{6,14},{7,15},{8,0},{9,1},... | collective-permute-start | bytes 1658888 | tf_op jit(solution)/shard_map/ppermute | solution.py:31
  526.1 61.4 %collective-permute-start.36 = (bf16[1280,384]{1,0:T(8,128)(2,1)}, bf16[1280,384]{1,0:T(8,128)(2,1)}, u32[]{:S(2)}, u32[]{:S(2)}) collective-permute-start(bf16[1280,384]{1,0:T(8,128)(2,1)} %get-tuple-element.153), channel_id=1, source_target_pairs={{0,16},{1,17},{2,18},{3,19},{4,20},{5,21},{6,22},{7,23},{8,24},{9,... | collective-permute-start | bytes 2949128 | tf_op jit(solution)/shard_map/ppermute | solution.py:31
  527.5 61.6 %collective-permute-start.35 = (bf16[1280,384]{1,0:T(8,128)(2,1)}, bf16[1280,384]{1,0:T(8,128)(2,1)}, u32[]{:S(2)}, u32[]{:S(2)}) collective-permute-start(bf16[1280,384]{1,0:T(8,128)(2,1)} %get-tuple-element.154), channel_id=1, source_target_pairs={{0,8},{1,9},{2,10},{3,11},{4,12},{5,13},{6,14},{7,15},{8,0},{9,1},... | collective-permute-start | bytes 2949128 | tf_op jit(solution)/shard_map/ppermute | solution.py:31
  531.0 71.3 %all-to-all-start.4 = ((bf16[4,80,3456]{2,1,0:T(8,128)(2,1)}), bf16[4,80,3456]{2,1,0:T(8,128)(2,1)S(1)}, u32[]{:S(2)}, u32[]{:S(2)}) async-start(bf16[4,80,3456]{2,1,0:T(8,128)(2,1)} %get-tuple-element.78), calls=%async_computation.4 | async-start | bytes 4423680 | tf_op jit(solution)/shard_map/all_to_all | solution.py:74
  546.8 117.9 %collective-permute-start.34 = (bf16[2048,384]{1,0:T(8,128)(2,1)}, bf16[2048,384]{1,0:T(8,128)(2,1)}, u32[]{:S(2)}, u32[]{:S(2)}) collective-permute-start(bf16[2048,384]{1,0:T(8,128)(2,1)} %get-tuple-element.156), channel_id=1, source_target_pairs={{0,1},{1,0},{2,3},{3,2},{4,5},{5,4},{6,7},{7,6},{8,9},{9,8},{10,11... | collective-permute-start | bytes 4718600 | tf_op jit(solution)/shard_map/ppermute | solution.py:31
  598.0 70.5 %collective-permute-start.38 = (bf16[2048,384]{1,0:T(8,128)(2,1)}, bf16[2048,384]{1,0:T(8,128)(2,1)}, u32[]{:S(2)}, u32[]{:S(2)}) collective-permute-start(bf16[2048,384]{1,0:T(8,128)(2,1)} %get-tuple-element.146), channel_id=1, source_target_pairs={{0,1},{1,0},{2,3},{3,2},{4,5},{5,4},{6,7},{7,6},{8,9},{9,8},{10,11... | collective-permute-start | bytes 4718600 | tf_op jit(solution)/shard_map/ppermute | solution.py:31
  602.3 56.2 %all-to-all-start.5 = ((bf16[4,80,3456]{2,1,0:T(8,128)(2,1)}), bf16[4,80,3456]{2,1,0:T(8,128)(2,1)}, u32[]{:S(2)}, u32[]{:S(2)}) async-start(bf16[4,80,3456]{2,1,0:T(8,128)(2,1)} %get-tuple-element.81), calls=%async_computation.5 | async-start | bytes 4423680 | tf_op jit(solution)/shard_map/all_to_all | solution.py:74
  (55 other events, 1219.8 us)
Sparse Core Ops, SparseCore 0:
  15.2 164.7 all-gather.9
  298.5 123.3 all-gather.11
  423.5 95.6 all-gather.13

commit v2 on v1

--- a/solution.py
+++ b/solution.py
@@ -37,6 +37,18 @@
 
 def pick(x, index, axis=0):
     return lax.dynamic_index_in_dim(x, index, axis, keepdims=False)
+
+
+def halves(x, rows, width):
+    upper = lax.reduce_precision(x, 8, 7)
+    pairs = jnp.stack([upper, x - upper]).astype(jnp.bfloat16).reshape(-1)
+    return jnp.pad(pairs, (0, rows * width - pairs.size)).reshape(rows, width)
+
+
+def unhalved(pairs, shape):
+    count = 2 * math.prod(shape)
+    pairs = pairs.reshape(-1)[:count].astype(jnp.float32)
+    return jnp.sum(pairs.reshape((2,) + tuple(shape)), axis=0)
 
 
 class Grid:
@@ -175,39 +187,36 @@
     )(info, query, *kv_pieces)
 
 
-def turn_kernel(width, x_ref, scale_ref, angle_ref, gain_ref, query_ref, kv_ref):
-    cosine = angle_ref[:, :HD]
-    sine = angle_ref[:, HD:]
-    for j, (out_ref, base) in enumerate(((query_ref, 0), (kv_ref, 0))):
-        scale = scale_ref[:, j : j + 1]
-        for at in range(0, width, HD):
-            x = x_ref[:, j * width + at : j * width + at + HD]
-            x = x * scale * gain_ref[j : j + 1, at : at + HD]
-            turned = x * cosine + pltpu.roll(x, HD // 2, 1) * sine
-            out_ref[:, at : at + HD] = turned.astype(out_ref.dtype)
-    kv_ref[:, width:] = x_ref[:, 2 * width :].astype(kv_ref.dtype)
+def turn_kernel(width, step, x_ref, scale_ref, angle_ref, gain_ref, query_ref, kv_ref):
+    def block(b, carry):
+        rows = pl.ds(pl.multiple_of(b * step, step), step)
+        cosine = angle_ref[rows, :HD]
+        sine = angle_ref[rows, HD:]
+        for j, out_ref in enumerate((query_ref, kv_ref)):
+            scale = scale_ref[rows, j : j + 1]
+            for at in range(0, width, HD):
+                x = x_ref[rows, j * width + at : j * width + at + HD]
+                x = x * scale * gain_ref[j : j + 1, at : at + HD]
+                turned = x * cosine + pltpu.roll(x, HD // 2, 1) * sine
+                out_ref[rows, at : at + HD] = turned.astype(out_ref.dtype)
+        kv_ref[rows, width:] = x_ref[rows, 2 * width :].astype(kv_ref.dtype)
+        return carry
+
+    lax.fori_loop(0, x_ref.shape[0] // step, block, 0)
 
 
 def turn(projected, scales, angles, gain):
     rows, width = projected.shape[0], projected.shape[1] // 3
-    step = 160 if rows % 160 == 0 else rows
+    whole = pl.BlockSpec(memory_space=pltpu.VMEM)
     return pl.pallas_call(
-        functools.partial(turn_kernel, width),
-        grid=(rows // step,),
-        in_specs=[
-            pl.BlockSpec((step, 3 * width), lambda b: (b, 0)),
-            pl.BlockSpec((step, 2), lambda b: (b, 0)),
-            pl.BlockSpec((step, 2 * HD), lambda b: (b, 0)),
-            pl.BlockSpec((2, width), lambda b: (0, 0)),
-        ],
-        out_specs=[
-            pl.BlockSpec((step, width), lambda b: (b, 0)),
-            pl.BlockSpec((step, 2 * width), lambda b: (b, 0)),
-        ],
+        functools.partial(turn_kernel, width, 80 if rows % 80 == 0 else rows),
+        in_specs=[whole] * 4,
+        out_specs=[whole] * 2,
         out_shape=[
             jax.ShapeDtypeStruct((rows, width), jnp.bfloat16),
             jax.ShapeDtypeStruct((rows, 2 * width), jnp.bfloat16),
         ],
+        compiler_params=pltpu.CompilerParams(vmem_limit_bytes=32 * 1024 * 1024),
         cost_estimate=pl.CostEstimate(
             flops=10 * rows * width, bytes_accessed=18 * rows * width, transcendentals=0
         ),
@@ -265,47 +274,45 @@
     quarter = lax.dynamic_slice_in_dim(hidden, row * part, part, 0).reshape(part, n_row, row_width)
     quarter = jnp.concatenate([pick(quarter, row ^ i, 1) for i in range(n_row)], axis=1)
     gathered = lax.all_gather(quarter, "col", axis=0, tiled=True)
-    gain = lax.all_gather(qk_gain, "row", axis=0)
-    weights = qkv_train.astype(bf16).transpose(1, 0, 2).reshape(row_width, 3 * units)
-    weights, gain = together(weights, gain)
-    gain = pick(gain, plane)
-    weight_pieces = grid.gather_row(weights)
-
-    def swap_cores(blocks, axis):
-        other = grid.other_core(pick(blocks, 1 - core, axis))
-        return pick(blocks, core, axis), other
-
-    qkv_blocks = grid.join_cores(
-        *swap_cores(weights.reshape(planes, 2, col_block, 3, units), 1), 3
-    ).reshape(planes, col_block, 6 * units)
-    ff = gate_up_train.astype(bf16).reshape(2, planes, 2, col_block, ff_units)
-    ff_blocks = grid.join_cores(*swap_cores(ff, 2), 3)
-    split = 2 if (col_block // 2) % 16 == 0 else 1
-    step_rows = col_block // split
-    chunks = [
-        ff_blocks[j, :, s * step_rows : (s + 1) * step_rows]
-        for j in range(2)
-        for s in range(split)
-    ]
-    at_planes = [grid.over_planes(chunks[0])]
-
     head_rows = o_weight.shape[0] // 2
     half_rows = lax.dynamic_slice_in_dim(o_weight, core * head_rows, head_rows, 0)
     columns = [
         lax.dynamic_slice_in_dim(half_rows, (row ^ i) * row_width, row_width, 1)
         for i in range(n_row)
     ]
-    all_weights, *columns = together(jnp.concatenate(weight_pieces, axis=0), *columns)
+    weights = qkv_train.astype(bf16).transpose(1, 0, 2).reshape(row_width, 3 * units)
+    weights, columns, gate_up_train = together(weights, columns, gate_up_train)
     columns = [columns[0]] + [grid.row_xor(columns[i], i) for i in range(1, n_row)]
-    gathered, at_planes[0], qkv_blocks = together(gathered, at_planes[0], qkv_blocks)
-    at_planes_qkv = grid.over_planes(qkv_blocks)
-    at_rows = [grid.over_rows(at_planes[0])]
+    gain_halves = halves(qk_gain, row_width // 40, 3 * units)
+    weight_pieces = grid.gather_row(jnp.concatenate([weights, gain_halves], axis=0))
+    gain = jnp.stack([x[row_width:] for x in weight_pieces])
+    weight_pieces = [x[:row_width] for x in weight_pieces]
+
+    def swap_cores(blocks, axis):
+        other = grid.other_core(pick(blocks, 1 - core, axis))
+        return pick(blocks, core, axis), other
+
+    def ff_blocks(matrix):
+        blocks = matrix.astype(bf16).reshape(planes, 2, col_block, ff_units)
+        return grid.join_cores(*swap_cores(blocks, 1), 2)
+
+    gate_blocks, own_weights = together(ff_blocks(gate_up_train[0]), weights)
+    at_planes_gate = grid.over_planes(gate_blocks)
+    qkv_blocks = grid.join_cores(
+        *swap_cores(own_weights.reshape(planes, 2, col_block, 3, units), 1), 3
+    ).reshape(planes, col_block, 6 * units)
+    gathered, qkv_blocks, columns, gain = together(gathered, qkv_blocks, columns, gain)
+    columns = jnp.stack(columns)
+    columns_other = grid.other_core(columns)
+    gain = unhalved(pick(gain, plane ^ row), qk_gain.shape)
     whole_heads = units % HD == 0
     held = units if whole_heads else 2 * units
     if whole_heads:
         gain = lax.dynamic_slice_in_dim(gain, core * units, units, 1)
 
-    projected = jnp.dot(gathered, all_weights, preferred_element_type=jnp.float32)
+    projected = jnp.dot(
+        gathered, jnp.concatenate(weight_pieces, axis=0), preferred_element_type=jnp.float32
+    )
     rows_here = n_col * part
     squares = jnp.stack(
         [
@@ -314,6 +321,8 @@
         ]
     )
     squares = jnp.sum(lax.all_gather(squares, "col", axis=0), axis=0)
+    squares, at_planes_gate, qkv_blocks = together(squares, at_planes_gate, qkv_blocks)
+    at_planes_qkv = grid.over_planes(qkv_blocks)
     inverse = inverse_rms(squares, heads_width).T
     if not whole_heads:
         projected = projected.reshape(rows_here, 3, units)
@@ -334,12 +343,7 @@
     angles = jnp.concatenate([cosine, cosine, -sine, sine], axis=1)
     query, kv = turn(projected, inverse, angles, gain)
 
-    query, kv, at_planes_qkv, chunks[1], at_rows[0], columns = together(
-        query, kv, at_planes_qkv, chunks[1], at_rows[0], columns
-    )
-    columns = jnp.stack(columns)
-    columns_other = grid.other_core(columns)
-    at_planes.append(grid.over_planes(chunks[1]))
+    query, kv, columns_other = together(query, kv, columns_other)
     key_or_value = [
         lax.dynamic_slice_in_dim(kv, j * held + core * units, units, 1)
         if not whole_heads
@@ -359,23 +363,9 @@
         kv_pieces = [natural.reshape(n_col, tokens, 2 * held)]
         offsets = jnp.zeros((1,), jnp.int32)
     info = jnp.concatenate([prompt_ends, (row * part)[None], offsets]).astype(jnp.int32)
-    kv_pieces[-1], at_planes_qkv = together(kv_pieces[-1], at_planes_qkv)
-    at_rows_qkv = grid.over_rows(at_planes_qkv)
+    kv_pieces[-1], at_planes_gate = together(kv_pieces[-1], at_planes_gate)
+    at_rows_gate = grid.over_rows(at_planes_gate)
     attention = attend(query.reshape(n_col, part, held), kv_pieces, info, tokens, prompts)
-
-    attention, at_planes[1], key_planes, at_rows_qkv, columns_other = together(
-        attention, at_planes[1], key_planes, at_rows_qkv, columns_other
-    )
-    at_rows.append(grid.over_rows(at_planes[1]))
-    key_rows = lax.all_to_all(key_planes, "row", split_axis=0, concat_axis=0, tiled=True)
-
-    def place_rows(whole, first, parts):
-        for at, blocks in enumerate(parts, first):
-            j, s = divmod(at, split)
-            whole = lax.dynamic_update_slice(
-                whole, jnp.stack(blocks)[None], (j, 0, s * step_rows, 0)
-            )
-        return whole
 
     attention = attention.reshape(planes, 2, part, held)
     mine = pick(attention, core, 1)
@@ -383,17 +373,20 @@
         attention = grid.join_cores(mine, grid.other_core(pick(attention, 1 - core, 1)), 2)
     else:
         attention = mine
-    arrived = jnp.stack(
-        [pick(attention, plane)]
-        + [
-            grid.move(pick(attention, plane ^ i), lambda r, c: (r, c ^ (2 * i)))
-            for i in range(1, planes)
-        ]
-    )
-    arrived, key_rows, chunks[2:3], at_rows[1], value_planes = together(
-        arrived, key_rows, chunks[2:3], at_rows[1], value_planes
-    )
-    at_planes += [grid.over_planes(chunk) for chunk in chunks[2:3]]
+    attention, key_planes, at_planes_qkv, at_rows_gate, gate_up_train = together(
+        attention, key_planes, at_planes_qkv, at_rows_gate, gate_up_train
+    )
+    arrived = grid.over_planes(attention)
+    key_rows = grid.over_rows(key_planes)
+    at_rows_qkv = grid.over_rows(at_planes_qkv)
+    up_blocks = ff_blocks(gate_up_train[1])
+    up_cut = col_block * 4 // 5
+    up_blocks, last_blocks = up_blocks[:, :up_cut], up_blocks[:, up_cut:]
+    arrived, key_rows, at_rows_qkv, value_planes, up_blocks, last_blocks = together(
+        arrived, key_rows, at_rows_qkv, value_planes, up_blocks, last_blocks
+    )
+    at_planes_up = grid.over_planes(up_blocks)
+    value_rows = grid.over_rows(value_planes)
     o_columns = jnp.concatenate(
         [
             grid.join_cores(pick(columns, row ^ r), pick(columns_other, row ^ r), 0)
@@ -401,33 +394,21 @@
         ],
         axis=0,
     )
-    ff_server = jnp.zeros((2, n_row, col_block, 2 * ff_units), bf16)
-    ff_server = place_rows(ff_server, 0, at_rows)
-    attention = jnp.concatenate([pick(arrived, h ^ plane) for h in range(planes)], axis=1)
+    attention = jnp.concatenate(list(arrived), axis=1)
     attention_rows = jnp.concatenate(grid.in_order(grid.gather_row(attention)), axis=0)
-    attention_rows, at_planes[2:], chunks[3:] = together(
-        attention_rows, at_planes[2:], chunks[3:]
-    )
-    at_rows += [grid.over_rows(blocks) for blocks in at_planes[2:]]
-    at_planes += [grid.over_planes(chunk) for chunk in chunks[3:]]
-    value_rows = jnp.stack(grid.over_rows(value_planes))
+    attention_rows, at_planes_up, last_blocks, at_rows_gate = together(
+        attention_rows, at_planes_up, last_blocks, at_rows_gate
+    )
+    at_planes_last = grid.over_planes(last_blocks)
+    at_rows_up = grid.over_rows(at_planes_up)
     summed = jnp.dot(attention_rows, o_columns, preferred_element_type=jnp.float32)
-    out_squares = lax.psum(jnp.sum(summed * summed, axis=1), "row")
-    normalized = summed * inverse_rms(out_squares, width)[:, None] * post_gain
-    residual = lax.dynamic_slice_in_dim(hidden, row * row_width, row_width, 1).astype(jnp.float32)
-    layer_out = (residual + normalized).astype(bf16)
-    ff_server = place_rows(ff_server, 2, at_rows[2:])
-    layer_out, at_planes[3:], ff_server = together(layer_out, at_planes[3:], ff_server)
-    at_rows += [grid.over_rows(blocks) for blocks in at_planes[3:]]
-    ff_server = place_rows(ff_server, 3, at_rows[3:])
-
     most = PAGES * PAGE
 
     def start_of(owner_col):
         return jnp.sum(jnp.where(owner == owner_col, prompt_starts, 0))
 
     def window(rows):
-        rows = rows.reshape(n_row, n_col, part, units).transpose(1, 0, 2, 3)
+        rows = jnp.stack(rows).reshape(n_row, n_col, part, units).transpose(1, 0, 2, 3)
         rows = rows.reshape(n_col * tokens, units)
         rows = jnp.concatenate([rows, jnp.zeros((most, units), bf16)], axis=0)
         other = grid.other_core(lax.dynamic_slice_in_dim(rows, start_of(col ^ 1), most, 0))
@@ -443,11 +424,25 @@
         jnp.where(my_table[None, :] == page_index[:, None], page_index[None, :], 0), axis=1
     )
     page_of_slot = jnp.where(jnp.any(mine), page_of_slot, 0)
+    key_window, value_window = window(key_rows), window(value_rows)
+    def place_rows(whole, blocks, j, low):
+        return lax.dynamic_update_slice(whole, jnp.stack(blocks)[None], (j, 0, low, 0))
+
+    ff_server = jnp.zeros((2, n_row, col_block, 2 * ff_units), bf16)
+    ff_server = place_rows(ff_server, at_rows_gate, 0, 0)
     cache = place_pages(
-        window(key_rows),
-        window(value_rows),
+        key_window,
+        value_window,
         jnp.concatenate([page_of_slot, my_length[None]]).astype(jnp.int32),
     )
+    summed, cache, ff_server = together(summed, cache, ff_server)
+    out_squares = lax.psum(jnp.sum(summed * summed, axis=1), "row")
+    out_squares, at_planes_last = together(out_squares, at_planes_last)
+    ff_server = place_rows(ff_server, at_rows_up, 1, 0)
+    ff_server = place_rows(ff_server, grid.over_rows(at_planes_last), 1, up_cut)
+    normalized = summed * inverse_rms(out_squares, width)[:, None] * post_gain
+    residual = lax.dynamic_slice_in_dim(hidden, row * row_width, row_width, 1).astype(jnp.float32)
+    layer_out = (residual + normalized).astype(bf16)
 
     qkv_server = jnp.stack(at_rows_qkv).reshape(n_row, col_block, 3, 2 * units).transpose(2, 0, 1, 3)
     return (layer_out, cache[None], qkv_server, ff_server)

time: 705 us -> 664 us (0.942)
  waiting for transfers between devices: 232 us -> 151 us
  local copies, waits for them, and re-layouts: 152 us -> 197 us
  blocking collectives: 66.7 us -> 42.8 us
  Pallas kernels: 53.1 us -> 63 us
  starting transfers between devices: 70.7 us -> 63.2 us
  other arithmetic: 77.4 us -> 84.7 us
    slice x0 -> x9, local copies, waits for them, and re-layouts: none -> 37.1 us  [the longest x2 13.3 us: local(): gate_blocks, own_weights = together(ff_blocks(gate_up_train[0]), weights)]
    ppermute x42 -> x40, waiting for transfers between devices: 185 us -> 150 us  [permute(): return lax.ppermute(x, BOTH, pairs)]
    all_to_all x5, waiting for transfers between devices: 30.2 us -> 0.01 us  [over_planes(): lax.all_to_all(blocks, 'col', split_axis=0, concat_axis=0, tiled=True, ax...]
    all_gather x1, blocking collectives: 38.4 us -> 20.4 us  [local(): squares = jnp.sum(lax.all_gather(squares, 'col', axis=0), axis=0)]
    all_gather x2, waiting for transfers between devices: 16.9 us -> 0.74 us  [local(): lax.all_gather(x, 'col', axis=0, axis_index_groups=same_core)]
    pallas_call x1, Pallas kernels: 33 us -> 47.4 us  [attend(): pl.pallas_call(kernel, grid_spec=pltpu.PrefetchScalarGridSpec(num_scalar_...]
    all_gather x1 -> x0, blocking collectives: 9.49 us -> none  [local(): gain = lax.all_gather(qk_gain, 'row', axis=0)]
    unnamed x65 -> x70, local copies, waits for them, and re-layouts: 32.3 us -> 22.9 us
  transfers between devices with their start and end apart: 51 -> 48, of which waited for: 22 -> 18; matrix products, arithmetic and copies ran while one was open for 34% -> 45% of each run, Pallas kernels for 8% -> 10%
where the time goes in v2:
time: 664 us; the launch traced here: 653 us
  local copies, waits for them, and re-layouts  197 us (30%)
  waiting for transfers between devices  151 us (23%)
  other arithmetic  84.7 us (13%)
  starting transfers between devices  63.2 us (10%)
  Pallas kernels  63 us (9%)
  blocking collectives  42.8 us (6%)
  matrix products  32 us (5%)
  between operations  18.8 us (3%)
    ppermute x40, waiting for transfers between devices, permute(): return lax.ppermute(x, BOTH, pairs)  150 us
    pallas_call x1, Pallas kernels, attend(): pl.pallas_call(kernel, grid_spec=pltpu.PrefetchScalarGridSpec(num_scalar_...  47.4 us
    ppermute x40, starting transfers between devices, permute(): return lax.ppermute(x, BOTH, pairs)  41 us
    dynamic_slice x14, local copies, waits for them, and re-layouts, pick(): return lax.dynamic_index_in_dim(x, index, axis, keepdims=False)  29.6 us
    select_n x9, other arithmetic, join_cores(): jnp.where(self.core == 0, jnp.concatenate([mine, other], axis=axis), jnp....  29.6 us
    dot_general x1, matrix products, local(): jnp.dot(gathered, jnp.concatenate(weight_pieces, axis=0), preferred_eleme...  23.4 us
    squeeze x9, local copies, waits for them, and re-layouts, pick(): return lax.dynamic_index_in_dim(x, index, axis, keepdims=False)  23.3 us
    unnamed x70, local copies, waits for them, and re-layouts  22.9 us
  transfers between devices with their start and end apart: 48, of which 18 were waited for; matrix products, arithmetic and copies ran while one was open for 45% of the time, Pallas kernels for 10%

profile of v2, /device:TPU:0, one launch (start us, length us, event | category | flops | bytes accessed | tf_op | source)
XLA Modules:
  0.0 652.6 jit_solution(3652602937475486676)
XLA Ops:
  19.8 7.6 %fusion.31 = (bf16[384,1280]{1,0:T(8,128)(2,1)}, bf16[384,1280]{1,0:T(8,128)(2,1)}, bf16[384,1280]{1,0:T(8,128)(2,1)}, bf16[384,1280]{1,0:T(8,128)(2,1)}) fusion(bf16[768,5120]{1,0:T(8,128)(2,1)} %param.15, s32[]{:T(128)S(6)} %select_n.255, s32[]{:T(128)S(6)} %select_n.262, s32[]{:T(128)S(6)} %select_n.258, s32[]{:T(128)S(6)} %select_n.256, s32[]{:T(128)S(6)} %select_n.260), kind=kLoop, calls=%fused_computation.184 | loop fusion | bytes 7864340 | tf_op jit(solution)/shard_map/dynamic_slice | solution.py:280
  39.9 6.2 slice.121
  46.0 7.2 %copy.108 = bf16[1,1280,1728]{2,1,0:T(8,128)(2,1)} copy(bf16[1,1280,1728]{1,2,0:T(8,128)(2,1)} %slice.121) | data formatting | bytes 8847360 | tf_op jit(solution)/shard_map/slice | solution.py:299
  63.1 9.5 %maximum_select_fusion = bf16[4,160,3456]{2,1,0:T(8,128)(2,1)} fusion(bf16[4,160,1728]{2,1,0:T(8,128)(2,1)} %collective-permute-done, bf16[4,160,1728]{2,1,0:T(8,128)(2,1)} %get-tuple-element.159, pred[]{:T(512)S(6)} %eq.18), kind=kLoop, calls=%fused_computation.23 | loop fusion | flops 19906560 | bytes 8847361 | tf_op jit(solution)/shard_map/jit(_where)/select_n | solution.py:101
  75.9 7.5 %reshape.154 = bf16[4,2,160,3,384]{4,3,2,1,0:T(4,128)(2,1)} reshape(bf16[1280,1152]{1,0:T(8,128)(2,1)} %copy.109) | data formatting | bytes 5898240 | tf_op jit(solution)/shard_map/reshape | solution.py:302
  89.6 15.4 %collective-permute-done.6 = bf16[1312,1152]{1,0:T(8,128)(2,1)} collective-permute-done((bf16[1312,1152]{1,0:T(8,128)(2,1)}, bf16[1312,1152]{1,0:T(8,128)(2,1)}, u32[]{:S(2)}, u32[]{:S(2)}) %collective-permute-start.6) | collective-permute-done | bytes 3022880 | tf_op jit(solution)/shard_map/ppermute | solution.py:31
  153.0 7.5 %collective-permute-done.7 = bf16[656,1152]{1,0:T(8,128)(2,1)} collective-permute-done((bf16[656,1152]{1,0:T(8,128)(2,1)}, bf16[656,1152]{1,0:T(8,128)(2,1)}, u32[]{:S(2)}, u32[]{:S(2)}) %collective-permute-start.7) | collective-permute-done | bytes 1511456 | tf_op jit(solution)/shard_map/ppermute | solution.py:31
  169.7 10.0 %collective-permute-done.4 = bf16[384,1280]{1,0:T(8,128)(2,1)} collective-permute-done((bf16[384,1280]{1,0:T(8,128)(2,1)S(1)}, bf16[384,1280]{1,0:T(8,128)(2,1)}, u32[]{:S(2)}, u32[]{:S(2)}) %collective-permute-start.4) | collective-permute-done | bytes 983072 | tf_op jit(solution)/shard_map/ppermute | solution.py:31
  183.3 23.4 %fusion.1 = f32[1280,1152]{0,1:T(8,128)} fusion(bf16[1280,5120]{1,0:T(8,128)(2,1)} %all-gather.8.cloned.1.call-done, bf16[656,1152]{0,1:T(8,128)(2,1)} %copy.119, bf16[656,1152]{0,1:T(8,128)(2,1)} %copy.118, bf16[1280,1152]{0,1:T(8,128)(2,1)} %copy.131, bf16[1280,1152]{0,1:T(8,128)(2,1)} %copy.130, bf16[1280,1152]{0,1:T(8,128)(2,1)} %bitcast.221), kind=kOutput, calls=%fused_computation.2 | convolution fusion | flops 15158476800 | bytes 30875648 | tf_op jit(solution)/shard_map/dot_general | solution.py:313
  206.7 7.7 %copy.122.x_ref = f32[1280,1152]{1,0:T(8,128)} copy(f32[1280,1152]{0,1:T(8,128)} %fusion.1) | data formatting | bytes 11796480 | tf_op jit(solution)/shard_map/dot_general | solution.py:313
  216.8 20.4 %all-gather.3 = f32[8,2,1280]{2,1,0:T(2,128)S(1)} all-gather(f32[1,2,1280]{2,1,0:T(2,128)S(1)} %maximum_bitcast_fusion.5), channel_id=2, replica_groups=mesh['row'=4,'col'=8] {'col'}, dimensions={0}, use_global_device_ids=true | all-gather | bytes 92160 | tf_op jit(solution)/shard_map/all_gather | solution.py:323
  256.8 36.0 %collective-permute-done.11 = bf16[1280,768]{1,0:T(8,128)(2,1)} collective-permute-done((bf16[1280,768]{1,0:T(8,128)(2,1)}, bf16[1280,768]{1,0:T(8,128)(2,1)}, u32[]{:S(2)}, u32[]{:S(2)}) %collective-permute-start.11) | collective-permute-done | bytes 1966112 | tf_op jit(solution)/shard_map/ppermute | solution.py:31
  312.8 5.7 collective-permute-done.13
  330.1 47.4 %attend.1 = bf16[8,160,384]{2,1,0:T(8,128)(2,1)S(1)} custom-call(s32[9]{0:T(128)S(1)} %concatenate.104.info, bf16[8,160,384]{2,1,0:T(8,128)(2,1)S(1)} %bitcast.218, bf16[8,160,768]{2,1,0:T(8,128)(2,1)S(1)} %bitcast.215, bf16[8,160,768]{2,1,0:T(8,128)(2,1)S(1)} %bitcast.217, bf16[8,160,768]{2,1,0:T(8,128)(2,1)} %bitcast.27.refs_2_, bf16[8,160,768]{2,1,0:T(8,128)(2,1)} %bitcast.241), custom_call_target="tpu_custom_call" | custom-call | flops 3774873600 | bytes 9830400 | tf_op jit(solution)/shard_map/attend/pallas_call | solution.py:170
  396.2 6.1 slice.120
  402.3 7.2 %copy.123 = bf16[1,1280,1728]{2,1,0:T(8,128)(2,1)} copy(bf16[1,1280,1728]{1,2,0:T(8,128)(2,1)} %slice.120) | data formatting | bytes 8847360 | tf_op jit(solution)/shard_map/slice | solution.py:382
  417.3 8.8 %collective-permute-done.22 = bf16[160,2304]{1,0:T(8,128)(2,1)} collective-permute-done((bf16[160,2304]{1,0:T(8,128)(2,1)}, bf16[160,2304]{1,0:T(8,128)(2,1)}, u32[]{:S(2)}, u32[]{:S(2)}) %collective-permute-start.22) | collective-permute-done | bytes 737312 | tf_op jit(solution)/shard_map/ppermute | solution.py:31
  436.5 11.6 %collective-permute-done.20 = bf16[1280,384]{1,0:T(8,128)(2,1)} collective-permute-done((bf16[1280,384]{1,0:T(8,128)(2,1)}, bf16[1280,384]{1,0:T(8,128)(2,1)}, u32[]{:S(2)}, u32[]{:S(2)}) %collective-permute-start.20) | collective-permute-done | bytes 983072 | tf_op jit(solution)/shard_map/ppermute | solution.py:31
  448.2 19.7 %collective-permute-done.19 = bf16[1280,384]{1,0:T(8,128)(2,1)} collective-permute-done((bf16[1280,384]{1,0:T(8,128)(2,1)}, bf16[1280,384]{1,0:T(8,128)(2,1)}, u32[]{:S(2)}, u32[]{:S(2)}) %collective-permute-start.19) | collective-permute-done | bytes 983072 | tf_op jit(solution)/shard_map/ppermute | solution.py:31
  472.1 6.6 %maximum_select_fusion.1 = bf16[4,160,3456]{2,1,0:T(8,128)(2,1)S(1)} fusion(bf16[4,160,1728]{2,1,0:T(8,128)(2,1)} %collective-permute-done.24, bf16[4,160,1728]{2,1,0:T(8,128)(2,1)S(1)} %get-tuple-element.157, pred[]{:T(512)S(6)} %eq.18), kind=kLoop, calls=%fused_computation.25 | loop fusion | flops 19906560 | bytes 8847361 | tf_op jit(solution)/shard_map/jit(_where)/select_n | solution.py:101
  533.1 18.0 %collective-permute-done.31 = bf16[1280,384]{1,0:T(8,128)(2,1)} collective-permute-done((bf16[1280,384]{1,0:T(8,128)(2,1)}, bf16[1280,384]{1,0:T(8,128)(2,1)}, u32[]{:S(2)}, u32[]{:S(2)}) %collective-permute-start.31) | collective-permute-done | bytes 983072 | tf_op jit(solution)/shard_map/ppermute | solution.py:31
  569.9 12.3 %place_pages.1 = bf16[16,2,128,768]{3,2,1,0:T(8,128)(2,1)} custom-call(s32[17]{0:T(128)} %pad_add_fusion.info, bf16[2048,768]{1,0:T(8,128)(2,1)} %maximum_select_fusion.2.key_ref, bf16[2048,768]{1,0:T(8,128)(2,1)} %maximum_select_fusion.3.value_ref), custom_call_target="tpu_custom_call" | custom-call | flops 3145728 | bytes 12582912 | tf_op jit(solution)/shard_map/place_pages/pallas_call | solution.py:239
  587.7 8.6 %fusion.9 = f32[640,1280]{1,0:T(8,128)S(1)} fusion(bf16[640,3072]{1,0:T(8,128)(2,1)S(1)} %copy-done.9, bf16[768,1280]{1,0:T(8,128)(2,1)S(1)} %copy-done.24, bf16[768,1280]{1,0:T(8,128)(2,1)} %maximum_select_fusion.7, bf16[768,1280]{1,0:T(8,128)(2,1)} %maximum_select_fusion.6, bf16[768,1280]{1,0:T(8,128)(2,1)} %maximum_select_fusion.5), kind=kOutput, calls=%fused_computation.11 | convolution fusion | flops 5064622080 | bytes 15073280 | tf_op jit(solution)/shard_map/dot_general | solution.py:404
  605.7 22.4 %psum.7 = f32[640]{0:T(1024)S(1)} all-reduce(f32[640]{0:T(1024)S(1)} %multiply_reduce_fusion), channel_id=1, replica_groups=mesh['row'=4,'col'=8] {'row'}, use_global_device_ids=true, to_apply=%region_13.14 | all-reduce | flops 640 | bytes 5120 | tf_op jit(solution)/shard_map/psum | solution.py:439
  (279 shorter events, 301.1 us)
Async XLA Ops:
  7.2 172.6 %all-gather.8.cloned.1.call-start = ((), (), s32[]{:S(2)}) async-start(), calls=%async_computation.5 | async-start | bytes 14745600 | tf_op jit(solution)/shard_map/all_gather | solution.py:276
  35.3 69.7 %collective-permute-start.6 = (bf16[1312,1152]{1,0:T(8,128)(2,1)}, bf16[1312,1152]{1,0:T(8,128)(2,1)}, u32[]{:S(2)}, u32[]{:S(2)}) collective-permute-start(bf16[1312,1152]{1,0:T(8,128)(2,1)} %copy.114), channel_id=1, source_target_pairs={{0,16},{1,17},{2,18},{3,19},{4,20},{5,21},{6,22},{7,23},{8,24},{9,... | collective-permute-start | bytes 9068552 | tf_op jit(solution)/shard_map/ppermute | solution.py:31
  38.4 71.3 %collective-permute-start.5 = (bf16[1312,1152]{1,0:T(8,128)(2,1)}, bf16[1312,1152]{1,0:T(8,128)(2,1)}, u32[]{:S(2)}, u32[]{:S(2)}) collective-permute-start(bf16[1312,1152]{1,0:T(8,128)(2,1)} %copy.114), channel_id=1, source_target_pairs={{0,8},{1,9},{2,10},{3,11},{4,12},{5,13},{6,14},{7,15},{8,0},{9,1},... | collective-permute-start | bytes 9068552 | tf_op jit(solution)/shard_map/ppermute | solution.py:31
  58.1 111.7 %collective-permute-start.2 = (bf16[384,1280]{1,0:T(8,128)(2,1)}, bf16[384,1280]{1,0:T(8,128)(2,1)}, u32[]{:S(2)}, u32[]{:S(2)}) collective-permute-start(bf16[384,1280]{1,0:T(8,128)(2,1)} %get-tuple-element.65), channel_id=1, source_target_pairs={{0,8},{1,9},{2,10},{3,11},{4,12},{5,13},{6,14},{7,15},{8,0},{9,1},... | collective-permute-start | bytes 2949128 | tf_op jit(solution)/shard_map/ppermute | solution.py:31
  58.6 111.1 %collective-permute-start.3 = (bf16[384,1280]{1,0:T(8,128)(2,1)}, bf16[384,1280]{1,0:T(8,128)(2,1)}, u32[]{:S(2)}, u32[]{:S(2)}) collective-permute-start(bf16[384,1280]{1,0:T(8,128)(2,1)} %get-tuple-element.66), channel_id=1, source_target_pairs={{0,16},{1,17},{2,18},{3,19},{4,20},{5,21},{6,22},{7,23},{8,24},{9,... | collective-permute-start | bytes 2949128 | tf_op jit(solution)/shard_map/ppermute | solution.py:31
  89.5 57.8 %collective-permute-start.1 = (bf16[4,160,3,384]{3,1,2,0:T(8,128)(2,1)}, bf16[4,160,3,384]{3,1,2,0:T(8,128)(2,1)}, u32[]{:S(2)}, u32[]{:S(2)}) collective-permute-start(bf16[4,160,3,384]{3,1,2,0:T(8,128)(2,1)} %bitcast.212), channel_id=1, source_target_pairs={{0,1},{1,0},{2,3},{3,2},{4,5},{5,4},{6,7},{7,6},{8,9},{9,8},{10,11... | collective-permute-start | bytes 4423688 | tf_op jit(solution)/shard_map/ppermute | solution.py:31
  107.7 52.9 %collective-permute-start.7 = (bf16[656,1152]{1,0:T(8,128)(2,1)}, bf16[656,1152]{1,0:T(8,128)(2,1)}, u32[]{:S(2)}, u32[]{:S(2)}) collective-permute-start(bf16[656,1152]{1,0:T(8,128)(2,1)} %slice.93), channel_id=1, source_target_pairs={{0,8},{1,9},{2,10},{3,11},{4,12},{5,13},{6,14},{7,15},{8,0},{9,1},... | collective-permute-start | bytes 4534280 | tf_op jit(solution)/shard_map/ppermute | solution.py:31
  112.3 52.0 %collective-permute-start.8 = (bf16[656,1152]{1,0:T(8,128)(2,1)}, bf16[656,1152]{1,0:T(8,128)(2,1)}, u32[]{:S(2)}, u32[]{:S(2)}) collective-permute-start(bf16[656,1152]{1,0:T(8,128)(2,1)} %slice.97), channel_id=1, source_target_pairs={{0,16},{1,17},{2,18},{3,19},{4,20},{5,21},{6,22},{7,23},{8,24},{9,... | collective-permute-start | bytes 4534280 | tf_op jit(solution)/shard_map/ppermute | solution.py:31
  122.1 115.2 %all-to-all-start = ((bf16[4,160,3456]{2,1,0:T(8,128)(2,1)}), bf16[4,160,3456]{2,1,0:T(8,128)(2,1)}, u32[]{:S(2)}, u32[]{:S(2)}) async-start(bf16[4,160,3456]{2,1,0:T(8,128)(2,1)} %maximum_select_fusion), calls=%async_computation | async-start | bytes 8847360 | tf_op jit(solution)/shard_map/all_to_all | solution.py:86
  127.3 259.9 %all-gather.10.cloned.1.call-start = ((), (), s32[]{:S(2)}) async-start(), calls=%async_computation.6 | async-start | bytes 4915200 | tf_op jit(solution)/shard_map/all_gather | solution.py:355
  183.3 61.3 %collective-permute-start.9 = (bf16[4,384,1280]{2,1,0:T(8,128)(2,1)}, bf16[4,384,1280]{2,1,0:T(8,128)(2,1)}, u32[]{:S(2)}, u32[]{:S(2)}) collective-permute-start(bf16[4,384,1280]{2,1,0:T(8,128)(2,1)} %pad_maximum_fusion.2), channel_id=1, source_target_pairs={{0,1},{1,0},{2,3},{3,2},{4,5},{5,4},{6,7},{7,6},{8,9},{9,8},{10,11... | collective-permute-start | bytes 11796488 | tf_op jit(solution)/shard_map/ppermute | solution.py:31
  247.4 45.4 %collective-permute-start.11 = (bf16[1280,768]{1,0:T(8,128)(2,1)}, bf16[1280,768]{1,0:T(8,128)(2,1)}, u32[]{:S(2)}, u32[]{:S(2)}) collective-permute-start(bf16[1280,768]{1,0:T(8,128)(2,1)} %copy-done.1), channel_id=1, source_target_pairs={{0,16},{1,17},{2,18},{3,19},{4,20},{5,21},{6,22},{7,23},{8,24},{9,... | collective-permute-start | bytes 5898248 | tf_op jit(solution)/shard_map/ppermute | solution.py:31
  249.1 47.6 %collective-permute-start.10 = (bf16[1280,768]{1,0:T(8,128)(2,1)}, bf16[1280,768]{1,0:T(8,128)(2,1)S(1)}, u32[]{:S(2)}, u32[]{:S(2)}) collective-permute-start(bf16[1280,768]{1,0:T(8,128)(2,1)} %copy-done.1), channel_id=1, source_target_pairs={{0,8},{1,9},{2,10},{3,11},{4,12},{5,13},{6,14},{7,15},{8,0},{9,1},... | collective-permute-start | bytes 5898248 | tf_op jit(solution)/shard_map/ppermute | solution.py:31
  251.5 135.7 %all-to-all-start.1 = ((bf16[4,160,2304]{2,1,0:T(8,128)(2,1)}), bf16[4,160,2304]{2,1,0:T(8,128)(2,1)}, u32[]{:S(2)}, u32[]{:S(2)}) async-start(bf16[4,160,2304]{2,1,0:T(8,128)(2,1)} %bitcast.227), calls=%async_computation.1 | async-start | bytes 5898240 | tf_op jit(solution)/shard_map/all_to_all | solution.py:86
  256.1 226.3 %all-gather.12.cloned.1.call-start = ((), (), s32[]{:S(2)}) async-start(), calls=%async_computation.7 | async-start | bytes 4915200 | tf_op jit(solution)/shard_map/all_gather | solution.py:355
  326.6 56.6 %collective-permute-start.17 = (bf16[160,3456]{1,0:T(8,128)(2,1)S(1)}, bf16[160,3456]{1,0:T(8,128)(2,1)S(1)}, u32[]{:S(2)}, u32[]{:S(2)}) collective-permute-start(bf16[160,3456]{1,0:T(8,128)(2,1)S(1)} %get-tuple-element.166), channel_id=1, source_target_pairs={{0,24},{1,25},{2,26},{3,27},{4,28},{5,29},{6,30},{7,31},{8,16},{9,... | collective-permute-start | bytes 3317768 | tf_op jit(solution)/shard_map/ppermute | solution.py:31
  328.1 55.1 %collective-permute-start.16 = (bf16[160,3456]{1,0:T(8,128)(2,1)S(1)}, bf16[160,3456]{1,0:T(8,128)(2,1)S(1)}, u32[]{:S(2)}, u32[]{:S(2)}) collective-permute-start(bf16[160,3456]{1,0:T(8,128)(2,1)S(1)} %get-tuple-element.167), channel_id=1, source_target_pairs={{0,16},{1,17},{2,18},{3,19},{4,20},{5,21},{6,22},{7,23},{8,24},{9,... | collective-permute-start | bytes 3317768 | tf_op jit(solution)/shard_map/ppermute | solution.py:31
  328.4 54.7 %collective-permute-start.15 = (bf16[160,3456]{1,0:T(8,128)(2,1)S(1)}, bf16[160,3456]{1,0:T(8,128)(2,1)}, u32[]{:S(2)}, u32[]{:S(2)}) collective-permute-start(bf16[160,3456]{1,0:T(8,128)(2,1)S(1)} %get-tuple-element.168), channel_id=1, source_target_pairs={{0,8},{1,9},{2,10},{3,11},{4,12},{5,13},{6,14},{7,15},{8,0},{9,1},... | collective-permute-start | bytes 3317768 | tf_op jit(solution)/shard_map/ppermute | solution.py:31
  413.7 58.4 %collective-permute-start.24 = (bf16[4,160,1728]{2,1,0:T(8,128)(2,1)}, bf16[4,160,1728]{2,1,0:T(8,128)(2,1)}, u32[]{:S(2)}, u32[]{:S(2)}) collective-permute-start(bf16[4,160,1728]{2,1,0:T(8,128)(2,1)} %get-tuple-element.158), channel_id=1, source_target_pairs={{0,1},{1,0},{2,3},{3,2},{4,5},{5,4},{6,7},{7,6},{8,9},{9,8},{10,11... | collective-permute-start | bytes 6635528 | tf_op jit(solution)/shard_map/ppermute | solution.py:31
  416.0 51.8 %collective-permute-start.19 = (bf16[1280,384]{1,0:T(8,128)(2,1)}, bf16[1280,384]{1,0:T(8,128)(2,1)}, u32[]{:S(2)}, u32[]{:S(2)}) collective-permute-start(bf16[1280,384]{1,0:T(8,128)(2,1)} %get-tuple-element.199), channel_id=1, source_target_pairs={{0,16},{1,17},{2,18},{3,19},{4,20},{5,21},{6,22},{7,23},{8,24},{9,... | collective-permute-start | bytes 2949128 | tf_op jit(solution)/shard_map/ppermute | solution.py:31
  428.7 53.7 %all-to-all-start.2 = ((bf16[4,160,768]{2,1,0:T(8,128)(2,1)}), bf16[4,160,768]{2,1,0:T(8,128)(2,1)S(1)}, u32[]{:S(2)}, u32[]{:S(2)}) async-start(bf16[4,160,768]{2,1,0:T(8,128)(2,1)} %maximum_select_fusion.9), calls=%async_computation.2 | async-start | bytes 1966080 | tf_op jit(solution)/shard_map/all_to_all | solution.py:86
  487.0 95.2 %all-to-all-start.3 = ((bf16[4,128,3456]{2,1,0:T(8,128)(2,1)}), bf16[4,128,3456]{2,1,0:T(8,128)(2,1)S(1)}, u32[]{:S(2)}, u32[]{:S(2)}) async-start(bf16[4,128,3456]{2,1,0:T(8,128)(2,1)} %slice.104), calls=%async_computation.3 | async-start | bytes 7077888 | tf_op jit(solution)/shard_map/all_to_all | solution.py:86
  495.7 55.4 %collective-permute-start.31 = (bf16[1280,384]{1,0:T(8,128)(2,1)}, bf16[1280,384]{1,0:T(8,128)(2,1)}, u32[]{:S(2)}, u32[]{:S(2)}) collective-permute-start(bf16[1280,384]{1,0:T(8,128)(2,1)} %get-tuple-element.177), channel_id=1, source_target_pairs={{0,16},{1,17},{2,18},{3,19},{4,20},{5,21},{6,22},{7,23},{8,24},{9,... | collective-permute-start | bytes 2949128 | tf_op jit(solution)/shard_map/ppermute | solution.py:31
  497.3 55.4 %collective-permute-start.30 = (bf16[1280,384]{1,0:T(8,128)(2,1)}, bf16[1280,384]{1,0:T(8,128)(2,1)}, u32[]{:S(2)}, u32[]{:S(2)}) collective-permute-start(bf16[1280,384]{1,0:T(8,128)(2,1)} %get-tuple-element.178), channel_id=1, source_target_pairs={{0,8},{1,9},{2,10},{3,11},{4,12},{5,13},{6,14},{7,15},{8,0},{9,1},... | collective-permute-start | bytes 2949128 | tf_op jit(solution)/shard_map/ppermute | solution.py:31
  (56 other events, 1040.1 us)
Sparse Core Ops, SparseCore 0:
  15.2 152.4 all-gather.7
  247.5 138.6 all-gather.9
  387.8 94.5 all-gather.11

commit v3 on v2

--- a/solution.py
+++ b/solution.py
@@ -396,12 +396,6 @@
     )
     attention = jnp.concatenate(list(arrived), axis=1)
     attention_rows = jnp.concatenate(grid.in_order(grid.gather_row(attention)), axis=0)
-    attention_rows, at_planes_up, last_blocks, at_rows_gate = together(
-        attention_rows, at_planes_up, last_blocks, at_rows_gate
-    )
-    at_planes_last = grid.over_planes(last_blocks)
-    at_rows_up = grid.over_rows(at_planes_up)
-    summed = jnp.dot(attention_rows, o_columns, preferred_element_type=jnp.float32)
     most = PAGES * PAGE
 
     def start_of(owner_col):
@@ -425,6 +419,12 @@
     )
     page_of_slot = jnp.where(jnp.any(mine), page_of_slot, 0)
     key_window, value_window = window(key_rows), window(value_rows)
+    attention_rows, at_planes_up, last_blocks, at_rows_gate, key_window, value_window = together(
+        attention_rows, at_planes_up, last_blocks, at_rows_gate, key_window, value_window
+    )
+    at_planes_last = grid.over_planes(last_blocks)
+    at_rows_up = grid.over_rows(at_planes_up)
+    summed = jnp.dot(attention_rows, o_columns, preferred_element_type=jnp.float32)
     def place_rows(whole, blocks, j, low):
         return lax.dynamic_update_slice(whole, jnp.stack(blocks)[None], (j, 0, low, 0))
 

time: 664 us -> 658 us (level)
  blocking collectives: 42.8 us -> 30.5 us
    psum x1, blocking collectives: 22.4 us -> 10.1 us  [local(): out_squares = lax.psum(jnp.sum(summed * summed, axis=1), 'row')]
where the time goes in v3:
time: 658 us; the launch traced here: 646 us
  local copies, waits for them, and re-layouts  197 us (30%)
  waiting for transfers between devices  157 us (24%)
  other arithmetic  84.5 us (13%)
  Pallas kernels  63 us (10%)
  starting transfers between devices  62.9 us (10%)
  matrix products  32.1 us (5%)
  blocking collectives  30.5 us (5%)
  between operations  18.8 us (3%)
    ppermute x40, waiting for transfers between devices, permute(): return lax.ppermute(x, BOTH, pairs)  151 us
    pallas_call x1, Pallas kernels, attend(): pl.pallas_call(kernel, grid_spec=pltpu.PrefetchScalarGridSpec(num_scalar_...  47.4 us
    ppermute x40, starting transfers between devices, permute(): return lax.ppermute(x, BOTH, pairs)  40.7 us
    dynamic_slice x14, local copies, waits for them, and re-layouts, pick(): return lax.dynamic_index_in_dim(x, index, axis, keepdims=False)  29.7 us
    select_n x9, other arithmetic, join_cores(): jnp.where(self.core == 0, jnp.concatenate([mine, other], axis=axis), jnp....  29.3 us
    dot_general x1, matrix products, local(): jnp.dot(gathered, jnp.concatenate(weight_pieces, axis=0), preferred_eleme...  23.4 us
    squeeze x9, local copies, waits for them, and re-layouts, pick(): return lax.dynamic_index_in_dim(x, index, axis, keepdims=False)  23.1 us
    unnamed x70, local copies, waits for them, and re-layouts  22.9 us
  transfers between devices with their start and end apart: 48, of which 18 were waited for; matrix products, arithmetic and copies ran while one was open for 45% of the time, Pallas kernels for 10%

profile of v3, /device:TPU:0, one launch (start us, length us, event | category | flops | bytes accessed | tf_op | source)
XLA Modules:
  0.0 645.8 jit_solution(3757970339540358322)
XLA Ops:
  19.8 7.6 %fusion.31 = (bf16[384,1280]{1,0:T(8,128)(2,1)}, bf16[384,1280]{1,0:T(8,128)(2,1)}, bf16[384,1280]{1,0:T(8,128)(2,1)}, bf16[384,1280]{1,0:T(8,128)(2,1)}) fusion(bf16[768,5120]{1,0:T(8,128)(2,1)} %param.15, s32[]{:T(128)S(6)} %select_n.255, s32[]{:T(128)S(6)} %select_n.262, s32[]{:T(128)S(6)} %select_n.258, s32[]{:T(128)S(6)} %select_n.256, s32[]{:T(128)S(6)} %select_n.260), kind=kLoop, calls=%fused_computation.184 | loop fusion | bytes 7864340 | tf_op jit(solution)/shard_map/dynamic_slice | solution.py:280
  39.9 6.2 slice.121
  46.0 7.2 %copy.108 = bf16[1,1280,1728]{2,1,0:T(8,128)(2,1)} copy(bf16[1,1280,1728]{1,2,0:T(8,128)(2,1)} %slice.121) | data formatting | bytes 8847360 | tf_op jit(solution)/shard_map/slice | solution.py:299
  63.1 9.5 %maximum_select_fusion = bf16[4,160,3456]{2,1,0:T(8,128)(2,1)} fusion(bf16[4,160,1728]{2,1,0:T(8,128)(2,1)} %collective-permute-done, bf16[4,160,1728]{2,1,0:T(8,128)(2,1)} %get-tuple-element.163, pred[]{:T(512)S(6)} %eq.18), kind=kLoop, calls=%fused_computation.23 | loop fusion | flops 19906560 | bytes 8847361 | tf_op jit(solution)/shard_map/jit(_where)/select_n | solution.py:101
  75.9 7.5 %reshape.154 = bf16[4,2,160,3,384]{4,3,2,1,0:T(4,128)(2,1)} reshape(bf16[1280,1152]{1,0:T(8,128)(2,1)} %copy.109) | data formatting | bytes 5898240 | tf_op jit(solution)/shard_map/reshape | solution.py:302
  89.6 15.4 %collective-permute-done.6 = bf16[1312,1152]{1,0:T(8,128)(2,1)} collective-permute-done((bf16[1312,1152]{1,0:T(8,128)(2,1)}, bf16[1312,1152]{1,0:T(8,128)(2,1)}, u32[]{:S(2)}, u32[]{:S(2)}) %collective-permute-start.6) | collective-permute-done | bytes 3022880 | tf_op jit(solution)/shard_map/ppermute | solution.py:31
  153.0 7.5 %collective-permute-done.7 = bf16[656,1152]{1,0:T(8,128)(2,1)} collective-permute-done((bf16[656,1152]{1,0:T(8,128)(2,1)}, bf16[656,1152]{1,0:T(8,128)(2,1)}, u32[]{:S(2)}, u32[]{:S(2)}) %collective-permute-start.7) | collective-permute-done | bytes 1511456 | tf_op jit(solution)/shard_map/ppermute | solution.py:31
  169.7 10.0 %collective-permute-done.4 = bf16[384,1280]{1,0:T(8,128)(2,1)} collective-permute-done((bf16[384,1280]{1,0:T(8,128)(2,1)S(1)}, bf16[384,1280]{1,0:T(8,128)(2,1)}, u32[]{:S(2)}, u32[]{:S(2)}) %collective-permute-start.4) | collective-permute-done | bytes 983072 | tf_op jit(solution)/shard_map/ppermute | solution.py:31
  183.3 23.4 %fusion.1 = f32[1280,1152]{0,1:T(8,128)} fusion(bf16[1280,5120]{1,0:T(8,128)(2,1)} %all-gather.8.cloned.1.call-done, bf16[656,1152]{0,1:T(8,128)(2,1)} %copy.119, bf16[656,1152]{0,1:T(8,128)(2,1)} %copy.118, bf16[1280,1152]{0,1:T(8,128)(2,1)} %copy.131, bf16[1280,1152]{0,1:T(8,128)(2,1)} %copy.130, bf16[1280,1152]{0,1:T(8,128)(2,1)} %bitcast.221), kind=kOutput, calls=%fused_computation.2 | convolution fusion | flops 15158476800 | bytes 30875648 | tf_op jit(solution)/shard_map/dot_general | solution.py:313
  206.7 7.7 %copy.122.x_ref = f32[1280,1152]{1,0:T(8,128)} copy(f32[1280,1152]{0,1:T(8,128)} %fusion.1) | data formatting | bytes 11796480 | tf_op jit(solution)/shard_map/dot_general | solution.py:313
  216.8 20.4 %all-gather.3 = f32[8,2,1280]{2,1,0:T(2,128)S(1)} all-gather(f32[1,2,1280]{2,1,0:T(2,128)S(1)} %maximum_bitcast_fusion.5), channel_id=2, replica_groups=mesh['row'=4,'col'=8] {'col'}, dimensions={0}, use_global_device_ids=true | all-gather | bytes 92160 | tf_op jit(solution)/shard_map/all_gather | solution.py:323
  256.8 36.0 %collective-permute-done.11 = bf16[1280,768]{1,0:T(8,128)(2,1)} collective-permute-done((bf16[1280,768]{1,0:T(8,128)(2,1)}, bf16[1280,768]{1,0:T(8,128)(2,1)}, u32[]{:S(2)}, u32[]{:S(2)}) %collective-permute-start.11) | collective-permute-done | bytes 1966112 | tf_op jit(solution)/shard_map/ppermute | solution.py:31
  312.8 5.7 collective-permute-done.13
  330.1 47.4 %attend.1 = bf16[8,160,384]{2,1,0:T(8,128)(2,1)S(1)} custom-call(s32[9]{0:T(128)S(1)} %concatenate.104.info, bf16[8,160,384]{2,1,0:T(8,128)(2,1)S(1)} %bitcast.218, bf16[8,160,768]{2,1,0:T(8,128)(2,1)S(1)} %bitcast.215, bf16[8,160,768]{2,1,0:T(8,128)(2,1)S(1)} %bitcast.217, bf16[8,160,768]{2,1,0:T(8,128)(2,1)} %bitcast.27.refs_2_, bf16[8,160,768]{2,1,0:T(8,128)(2,1)} %bitcast.241), custom_call_target="tpu_custom_call" | custom-call | flops 3774873600 | bytes 9830400 | tf_op jit(solution)/shard_map/attend/pallas_call | solution.py:170
  396.3 6.1 slice.120
  402.3 7.2 %copy.123 = bf16[1,1280,1728]{2,1,0:T(8,128)(2,1)} copy(bf16[1,1280,1728]{1,2,0:T(8,128)(2,1)} %slice.120) | data formatting | bytes 8847360 | tf_op jit(solution)/shard_map/slice | solution.py:382
  417.4 8.8 %collective-permute-done.22 = bf16[160,2304]{1,0:T(8,128)(2,1)} collective-permute-done((bf16[160,2304]{1,0:T(8,128)(2,1)}, bf16[160,2304]{1,0:T(8,128)(2,1)}, u32[]{:S(2)}, u32[]{:S(2)}) %collective-permute-start.22) | collective-permute-done | bytes 737312 | tf_op jit(solution)/shard_map/ppermute | solution.py:31
  436.5 11.7 %collective-permute-done.20 = bf16[1280,384]{1,0:T(8,128)(2,1)} collective-permute-done((bf16[1280,384]{1,0:T(8,128)(2,1)}, bf16[1280,384]{1,0:T(8,128)(2,1)}, u32[]{:S(2)}, u32[]{:S(2)}) %collective-permute-start.20) | collective-permute-done | bytes 983072 | tf_op jit(solution)/shard_map/ppermute | solution.py:31
  448.2 19.7 %collective-permute-done.19 = bf16[1280,384]{1,0:T(8,128)(2,1)} collective-permute-done((bf16[1280,384]{1,0:T(8,128)(2,1)}, bf16[1280,384]{1,0:T(8,128)(2,1)}, u32[]{:S(2)}, u32[]{:S(2)}) %collective-permute-start.19) | collective-permute-done | bytes 983072 | tf_op jit(solution)/shard_map/ppermute | solution.py:31
  472.0 6.4 maximum_select_fusion.1
  533.1 18.0 %collective-permute-done.31 = bf16[1280,384]{1,0:T(8,128)(2,1)} collective-permute-done((bf16[1280,384]{1,0:T(8,128)(2,1)}, bf16[1280,384]{1,0:T(8,128)(2,1)}, u32[]{:S(2)}, u32[]{:S(2)}) %collective-permute-start.31) | collective-permute-done | bytes 983072 | tf_op jit(solution)/shard_map/ppermute | solution.py:31
  575.5 8.6 %fusion.9 = f32[640,1280]{1,0:T(8,128)S(1)} fusion(bf16[640,3072]{1,0:T(8,128)(2,1)S(1)} %copy-done.9, bf16[768,1280]{1,0:T(8,128)(2,1)S(1)} %copy-done.24, bf16[768,1280]{1,0:T(8,128)(2,1)} %maximum_select_fusion.7, bf16[768,1280]{1,0:T(8,128)(2,1)} %maximum_select_fusion.6, bf16[768,1280]{1,0:T(8,128)(2,1)} %maximum_select_fusion.5), kind=kOutput, calls=%fused_computation.11 | convolution fusion | flops 5064622080 | bytes 15073280 | tf_op jit(solution)/shard_map/dot_general | solution.py:427
  589.0 12.3 %place_pages.1 = bf16[16,2,128,768]{3,2,1,0:T(8,128)(2,1)} custom-call(s32[17]{0:T(128)} %pad_add_fusion.info, bf16[2048,768]{1,0:T(8,128)(2,1)} %maximum_select_fusion.2.key_ref, bf16[2048,768]{1,0:T(8,128)(2,1)} %maximum_select_fusion.3.value_ref), custom_call_target="tpu_custom_call" | custom-call | flops 3145728 | bytes 12582912 | tf_op jit(solution)/shard_map/place_pages/pallas_call | solution.py:239
  605.8 10.1 %psum.7 = f32[640]{0:T(1024)S(1)} all-reduce(f32[640]{0:T(1024)S(1)} %multiply_reduce_fusion), channel_id=1, replica_groups=mesh['row'=4,'col'=8] {'row'}, use_global_device_ids=true, to_apply=%region_13.14 | all-reduce | flops 640 | bytes 5120 | tf_op jit(solution)/shard_map/psum | solution.py:439
  (279 shorter events, 306.6 us)
Async XLA Ops:
  7.2 172.6 %all-gather.8.cloned.1.call-start = ((), (), s32[]{:S(2)}) async-start(), calls=%async_computation.5 | async-start | bytes 14745600 | tf_op jit(solution)/shard_map/all_gather | solution.py:276
  35.3 69.7 %collective-permute-start.6 = (bf16[1312,1152]{1,0:T(8,128)(2,1)}, bf16[1312,1152]{1,0:T(8,128)(2,1)}, u32[]{:S(2)}, u32[]{:S(2)}) collective-permute-start(bf16[1312,1152]{1,0:T(8,128)(2,1)} %copy.114), channel_id=1, source_target_pairs={{0,16},{1,17},{2,18},{3,19},{4,20},{5,21},{6,22},{7,23},{8,24},{9,... | collective-permute-start | bytes 9068552 | tf_op jit(solution)/shard_map/ppermute | solution.py:31
  38.4 71.3 %collective-permute-start.5 = (bf16[1312,1152]{1,0:T(8,128)(2,1)}, bf16[1312,1152]{1,0:T(8,128)(2,1)}, u32[]{:S(2)}, u32[]{:S(2)}) collective-permute-start(bf16[1312,1152]{1,0:T(8,128)(2,1)} %copy.114), channel_id=1, source_target_pairs={{0,8},{1,9},{2,10},{3,11},{4,12},{5,13},{6,14},{7,15},{8,0},{9,1},... | collective-permute-start | bytes 9068552 | tf_op jit(solution)/shard_map/ppermute | solution.py:31
  58.1 111.7 %collective-permute-start.2 = (bf16[384,1280]{1,0:T(8,128)(2,1)}, bf16[384,1280]{1,0:T(8,128)(2,1)}, u32[]{:S(2)}, u32[]{:S(2)}) collective-permute-start(bf16[384,1280]{1,0:T(8,128)(2,1)} %get-tuple-element.67), channel_id=1, source_target_pairs={{0,8},{1,9},{2,10},{3,11},{4,12},{5,13},{6,14},{7,15},{8,0},{9,1},... | collective-permute-start | bytes 2949128 | tf_op jit(solution)/shard_map/ppermute | solution.py:31
  58.6 111.1 %collective-permute-start.3 = (bf16[384,1280]{1,0:T(8,128)(2,1)}, bf16[384,1280]{1,0:T(8,128)(2,1)}, u32[]{:S(2)}, u32[]{:S(2)}) collective-permute-start(bf16[384,1280]{1,0:T(8,128)(2,1)} %get-tuple-element.68), channel_id=1, source_target_pairs={{0,16},{1,17},{2,18},{3,19},{4,20},{5,21},{6,22},{7,23},{8,24},{9,... | collective-permute-start | bytes 2949128 | tf_op jit(solution)/shard_map/ppermute | solution.py:31
  89.5 57.8 %collective-permute-start.1 = (bf16[4,160,3,384]{3,1,2,0:T(8,128)(2,1)}, bf16[4,160,3,384]{3,1,2,0:T(8,128)(2,1)}, u32[]{:S(2)}, u32[]{:S(2)}) collective-permute-start(bf16[4,160,3,384]{3,1,2,0:T(8,128)(2,1)} %bitcast.212), channel_id=1, source_target_pairs={{0,1},{1,0},{2,3},{3,2},{4,5},{5,4},{6,7},{7,6},{8,9},{9,8},{10,11... | collective-permute-start | bytes 4423688 | tf_op jit(solution)/shard_map/ppermute | solution.py:31
  107.7 52.9 %collective-permute-start.7 = (bf16[656,1152]{1,0:T(8,128)(2,1)}, bf16[656,1152]{1,0:T(8,128)(2,1)}, u32[]{:S(2)}, u32[]{:S(2)}) collective-permute-start(bf16[656,1152]{1,0:T(8,128)(2,1)} %slice.93), channel_id=1, source_target_pairs={{0,8},{1,9},{2,10},{3,11},{4,12},{5,13},{6,14},{7,15},{8,0},{9,1},... | collective-permute-start | bytes 4534280 | tf_op jit(solution)/shard_map/ppermute | solution.py:31
  112.3 52.0 %collective-permute-start.8 = (bf16[656,1152]{1,0:T(8,128)(2,1)}, bf16[656,1152]{1,0:T(8,128)(2,1)}, u32[]{:S(2)}, u32[]{:S(2)}) collective-permute-start(bf16[656,1152]{1,0:T(8,128)(2,1)} %slice.97), channel_id=1, source_target_pairs={{0,16},{1,17},{2,18},{3,19},{4,20},{5,21},{6,22},{7,23},{8,24},{9,... | collective-permute-start | bytes 4534280 | tf_op jit(solution)/shard_map/ppermute | solution.py:31
  122.1 115.2 %all-to-all-start = ((bf16[4,160,3456]{2,1,0:T(8,128)(2,1)}), bf16[4,160,3456]{2,1,0:T(8,128)(2,1)}, u32[]{:S(2)}, u32[]{:S(2)}) async-start(bf16[4,160,3456]{2,1,0:T(8,128)(2,1)} %maximum_select_fusion), calls=%async_computation | async-start | bytes 8847360 | tf_op jit(solution)/shard_map/all_to_all | solution.py:86
  127.3 259.9 %all-gather.10.cloned.1.call-start = ((), (), s32[]{:S(2)}) async-start(), calls=%async_computation.6 | async-start | bytes 4915200 | tf_op jit(solution)/shard_map/all_gather | solution.py:355
  183.3 61.3 %collective-permute-start.9 = (bf16[4,384,1280]{2,1,0:T(8,128)(2,1)}, bf16[4,384,1280]{2,1,0:T(8,128)(2,1)}, u32[]{:S(2)}, u32[]{:S(2)}) collective-permute-start(bf16[4,384,1280]{2,1,0:T(8,128)(2,1)} %pad_maximum_fusion.2), channel_id=1, source_target_pairs={{0,1},{1,0},{2,3},{3,2},{4,5},{5,4},{6,7},{7,6},{8,9},{9,8},{10,11... | collective-permute-start | bytes 11796488 | tf_op jit(solution)/shard_map/ppermute | solution.py:31
  247.4 45.4 %collective-permute-start.11 = (bf16[1280,768]{1,0:T(8,128)(2,1)}, bf16[1280,768]{1,0:T(8,128)(2,1)}, u32[]{:S(2)}, u32[]{:S(2)}) collective-permute-start(bf16[1280,768]{1,0:T(8,128)(2,1)} %copy-done.1), channel_id=1, source_target_pairs={{0,16},{1,17},{2,18},{3,19},{4,20},{5,21},{6,22},{7,23},{8,24},{9,... | collective-permute-start | bytes 5898248 | tf_op jit(solution)/shard_map/ppermute | solution.py:31
  249.1 47.6 %collective-permute-start.10 = (bf16[1280,768]{1,0:T(8,128)(2,1)}, bf16[1280,768]{1,0:T(8,128)(2,1)S(1)}, u32[]{:S(2)}, u32[]{:S(2)}) collective-permute-start(bf16[1280,768]{1,0:T(8,128)(2,1)} %copy-done.1), channel_id=1, source_target_pairs={{0,8},{1,9},{2,10},{3,11},{4,12},{5,13},{6,14},{7,15},{8,0},{9,1},... | collective-permute-start | bytes 5898248 | tf_op jit(solution)/shard_map/ppermute | solution.py:31
  251.5 135.7 %all-to-all-start.1 = ((bf16[4,160,2304]{2,1,0:T(8,128)(2,1)}), bf16[4,160,2304]{2,1,0:T(8,128)(2,1)}, u32[]{:S(2)}, u32[]{:S(2)}) async-start(bf16[4,160,2304]{2,1,0:T(8,128)(2,1)} %bitcast.227), calls=%async_computation.1 | async-start | bytes 5898240 | tf_op jit(solution)/shard_map/all_to_all | solution.py:86
  256.1 226.3 %all-gather.12.cloned.1.call-start = ((), (), s32[]{:S(2)}) async-start(), calls=%async_computation.7 | async-start | bytes 4915200 | tf_op jit(solution)/shard_map/all_gather | solution.py:355
  326.6 56.6 %collective-permute-start.17 = (bf16[160,3456]{1,0:T(8,128)(2,1)S(1)}, bf16[160,3456]{1,0:T(8,128)(2,1)S(1)}, u32[]{:S(2)}, u32[]{:S(2)}) collective-permute-start(bf16[160,3456]{1,0:T(8,128)(2,1)S(1)} %get-tuple-element.170), channel_id=1, source_target_pairs={{0,24},{1,25},{2,26},{3,27},{4,28},{5,29},{6,30},{7,31},{8,16},{9,... | collective-permute-start | bytes 3317768 | tf_op jit(solution)/shard_map/ppermute | solution.py:31
  328.1 55.1 %collective-permute-start.16 = (bf16[160,3456]{1,0:T(8,128)(2,1)S(1)}, bf16[160,3456]{1,0:T(8,128)(2,1)S(1)}, u32[]{:S(2)}, u32[]{:S(2)}) collective-permute-start(bf16[160,3456]{1,0:T(8,128)(2,1)S(1)} %get-tuple-element.171), channel_id=1, source_target_pairs={{0,16},{1,17},{2,18},{3,19},{4,20},{5,21},{6,22},{7,23},{8,24},{9,... | collective-permute-start | bytes 3317768 | tf_op jit(solution)/shard_map/ppermute | solution.py:31
  328.4 54.7 %collective-permute-start.15 = (bf16[160,3456]{1,0:T(8,128)(2,1)S(1)}, bf16[160,3456]{1,0:T(8,128)(2,1)}, u32[]{:S(2)}, u32[]{:S(2)}) collective-permute-start(bf16[160,3456]{1,0:T(8,128)(2,1)S(1)} %get-tuple-element.172), channel_id=1, source_target_pairs={{0,8},{1,9},{2,10},{3,11},{4,12},{5,13},{6,14},{7,15},{8,0},{9,1},... | collective-permute-start | bytes 3317768 | tf_op jit(solution)/shard_map/ppermute | solution.py:31
  413.8 58.3 %collective-permute-start.24 = (bf16[4,160,1728]{2,1,0:T(8,128)(2,1)}, bf16[4,160,1728]{2,1,0:T(8,128)(2,1)}, u32[]{:S(2)}, u32[]{:S(2)}) collective-permute-start(bf16[4,160,1728]{2,1,0:T(8,128)(2,1)} %get-tuple-element.162), channel_id=1, source_target_pairs={{0,1},{1,0},{2,3},{3,2},{4,5},{5,4},{6,7},{7,6},{8,9},{9,8},{10,11... | collective-permute-start | bytes 6635528 | tf_op jit(solution)/shard_map/ppermute | solution.py:31
  416.1 51.8 %collective-permute-start.19 = (bf16[1280,384]{1,0:T(8,128)(2,1)}, bf16[1280,384]{1,0:T(8,128)(2,1)}, u32[]{:S(2)}, u32[]{:S(2)}) collective-permute-start(bf16[1280,384]{1,0:T(8,128)(2,1)} %get-tuple-element.203), channel_id=1, source_target_pairs={{0,16},{1,17},{2,18},{3,19},{4,20},{5,21},{6,22},{7,23},{8,24},{9,... | collective-permute-start | bytes 2949128 | tf_op jit(solution)/shard_map/ppermute | solution.py:31
  428.6 53.8 %all-to-all-start.2 = ((bf16[4,160,768]{2,1,0:T(8,128)(2,1)}), bf16[4,160,768]{2,1,0:T(8,128)(2,1)S(1)}, u32[]{:S(2)}, u32[]{:S(2)}) async-start(bf16[4,160,768]{2,1,0:T(8,128)(2,1)} %maximum_select_fusion.9), calls=%async_computation.2 | async-start | bytes 1966080 | tf_op jit(solution)/shard_map/all_to_all | solution.py:86
  487.0 83.0 %all-to-all-start.3 = ((bf16[4,128,3456]{2,1,0:T(8,128)(2,1)}), bf16[4,128,3456]{2,1,0:T(8,128)(2,1)S(1)}, u32[]{:S(2)}, u32[]{:S(2)}) async-start(bf16[4,128,3456]{2,1,0:T(8,128)(2,1)} %slice.104), calls=%async_computation.3 | async-start | bytes 7077888 | tf_op jit(solution)/shard_map/all_to_all | solution.py:86
  495.6 55.5 %collective-permute-start.31 = (bf16[1280,384]{1,0:T(8,128)(2,1)}, bf16[1280,384]{1,0:T(8,128)(2,1)}, u32[]{:S(2)}, u32[]{:S(2)}) collective-permute-start(bf16[1280,384]{1,0:T(8,128)(2,1)} %get-tuple-element.189), channel_id=1, source_target_pairs={{0,16},{1,17},{2,18},{3,19},{4,20},{5,21},{6,22},{7,23},{8,24},{9,... | collective-permute-start | bytes 2949128 | tf_op jit(solution)/shard_map/ppermute | solution.py:31
  497.1 55.6 %collective-permute-start.30 = (bf16[1280,384]{1,0:T(8,128)(2,1)}, bf16[1280,384]{1,0:T(8,128)(2,1)}, u32[]{:S(2)}, u32[]{:S(2)}) collective-permute-start(bf16[1280,384]{1,0:T(8,128)(2,1)} %get-tuple-element.190), channel_id=1, source_target_pairs={{0,8},{1,9},{2,10},{3,11},{4,12},{5,13},{6,14},{7,15},{8,0},{9,1},... | collective-permute-start | bytes 2949128 | tf_op jit(solution)/shard_map/ppermute | solution.py:31
  (56 other events, 1039.6 us)
Sparse Core Ops, SparseCore 0:
  15.2 152.4 all-gather.7
  247.5 138.6 all-gather.9
  387.8 94.5 all-gather.11
